TPU v7x, 512 devices: a whole 4x4x16 slice. The times are simulated.
512 devices in a mesh: ctx: 64 (over z, y_lo, core), head: 8 (over y_hi, x).
Axes of the slice: x: 4, y: 4 (y_hi: 2, y_lo: 2; y = y_hi * 2 + y_lo), z: 16, core: 2. Of those that a mesh axis runs over, the one named last changes fastest.
Arguments:
- queries: float32 [2, 64, 64, 128], P(None, 'ctx', 'head'), may hold values from -256 to 256
- prompt_keys: float32 [16384, 8, 128], P('ctx', 'head'), may hold values from -6 to 6
- prompt_values: float32 [16384, 8, 128], P('ctx', 'head'), may hold values from -6 to 6
- suffix_keys: float32 [64, 128, 8, 128], P('ctx', None, 'head'), may hold values from -8.4 to 8.4
- suffix_values: float32 [64, 128, 8, 128], P('ctx', None, 'head'), may hold values from -6 to 6
- new_keys: float32 [2, 64, 8, 128], P(None, 'ctx', 'head'), may hold values from -18 to 18
- new_values: float32 [2, 64, 8, 128], P(None, 'ctx', 'head'), may hold values from -6 to 6
- suffix_lengths: int32 [64], P('ctx'), may hold values from 1 to 128, as said below
- out_weight: float32 [8192, 5120], P('head', 'ctx'), may hold values from -0.0625 to 0.0625
Outputs:
- layer_out: float32 [2, 64, 5120], P(None, 'head', 'ctx')
Inputs may be any that keep to these rules, and one draw needn't show every extreme that they name: `suffix_lengths`: some row has exactly 128 live slots.
All inputs are finite; a program needn't handle non-finite values.
Results may differ from a plain program's by a relative error of at most 0.0003.
Values sent between devices are 32-bit elements; how exact they have to be, the bound alone decides.
A program may use at most 192 MiB of HBM per device.

v0:
```python
import jax
import jax.numpy as jnp
from jax import lax
from jax.sharding import PartitionSpec as P

HIGHEST = lax.Precision.HIGHEST


def from_behind(value, axis, steps):
    count = lax.axis_size(axis)
    pairs = [(source, (source + steps) % count) for source in range(count)]
    return lax.ppermute(value, axis, pairs)


def combine(first, second):
    peak_a, total_a, weighted_a = first
    peak_b, total_b, weighted_b = second
    row_peak = jnp.maximum(peak_a, peak_b)
    scale_a = jnp.exp(peak_a - row_peak)
    scale_b = jnp.exp(peak_b - row_peak)
    return (
        row_peak,
        total_a * scale_a + total_b * scale_b,
        weighted_a * scale_a[..., None] + weighted_b * scale_b[..., None],
    )


def prompt_part(query_block, key_rows, value_rows):
    score_scale = query_block.shape[-1] ** (-0.5)
    scores = jnp.einsum("trkgd,pkd->trkgp", query_block, key_rows, precision=HIGHEST) * score_scale
    row_peak = jnp.max(scores, axis=-1)
    weights = jnp.exp(scores - row_peak[..., None])
    row_total = jnp.sum(weights, axis=-1)
    weighted = jnp.einsum("trkgp,pkd->trkgd", weights, value_rows, precision=HIGHEST)
    return (row_peak, row_total, weighted)


def suffix_part(query_block, suf_keys, suf_values, fresh_keys, fresh_values, lengths):
    score_scale = query_block.shape[-1] ** (-0.5)
    slot_count = suf_keys.shape[1]
    step_count = query_block.shape[0]
    suf_scores = (
        jnp.einsum("trkgd,rskd->trkgs", query_block, suf_keys, precision=HIGHEST) * score_scale
    )
    live_slots = jnp.arange(slot_count, dtype=jnp.int32)[None, :] < lengths[:, None]
    suf_scores = jnp.where(live_slots[None, :, None, None, :], suf_scores, -1e30)
    new_scores = (
        jnp.einsum("trkgd,urkd->trkgu", query_block, fresh_keys, precision=HIGHEST) * score_scale
    )
    step_ids = jnp.arange(step_count, dtype=jnp.int32)
    new_mask = step_ids[None, :] <= step_ids[:, None]
    new_scores = jnp.where(new_mask[:, None, None, None, :], new_scores, -1e30)
    row_peak = jnp.maximum(jnp.max(suf_scores, axis=-1), jnp.max(new_scores, axis=-1))
    suf_weights = jnp.exp(suf_scores - row_peak[..., None])
    new_weights = jnp.exp(new_scores - row_peak[..., None])
    row_total = jnp.sum(suf_weights, axis=-1) + jnp.sum(new_weights, axis=-1)
    weighted = jnp.einsum(
        "trkgs,rskd->trkgd", suf_weights, suf_values, precision=HIGHEST
    ) + jnp.einsum("trkgu,urkd->trkgd", new_weights, fresh_values, precision=HIGHEST)
    return (row_peak, row_total, weighted)


def local(
    queries,
    prompt_keys,
    prompt_values,
    suffix_keys,
    suffix_values,
    new_keys,
    new_values,
    suffix_lengths,
    out_weight,
):
    step_count, row_count, head_count, head_width = queries.shape
    kv_local = prompt_keys.shape[1]
    group_size = head_count // kv_local
    query_block = queries.reshape(step_count, row_count, kv_local, group_size, head_width)
    suffix_parts = suffix_part(
        query_block, suffix_keys, suffix_values, new_keys, new_values, suffix_lengths
    )

    def visit(cycle_step, carry):
        moving, row_peak, row_total, weighted = carry
        row_peak, row_total, weighted = combine(
            (row_peak, row_total, weighted), prompt_part(moving, prompt_keys, prompt_values)
        )
        return from_behind((moving, row_peak, row_total, weighted), "ctx", 1)

    moving, row_peak, row_total, weighted = lax.fori_loop(
        0, lax.axis_size("ctx"), visit, (query_block,) + suffix_parts
    )
    attention = (weighted / row_total[..., None]).reshape(
        step_count, row_count, head_count * head_width
    )
    partial_out = jnp.einsum(
        "hnq,qm->hnm",
        lax.all_gather(attention, "ctx", axis=1, tiled=True),
        out_weight,
        precision=HIGHEST,
    )
    return lax.psum_scatter(partial_out, "head", scatter_dimension=1, tiled=True)


def solution(mesh):
    return jax.shard_map(
        local,
        mesh=mesh,
        in_specs=(
            P(None, "ctx", "head", None),
            P("ctx", "head", None),
            P("ctx", "head", None),
            P("ctx", None, "head", None),
            P("ctx", None, "head", None),
            P(None, "ctx", "head", None),
            P(None, "ctx", "head", None),
            P("ctx"),
            P("head", "ctx"),
        ),
        out_specs=P(None, "head", "ctx"),
        check_vma=False,
    )
```

profile of v0, /device:TPU:1, one launch (start us, length us, event | category | flops | bytes accessed | tf_op | source)
XLA Modules:
  0.0 1039.4 jit_solution(704873618248989195)
XLA Ops:
  10.9 882.7 %while.16 = (s32[]{:T(128)}, f32[2,1,1,8,128]{4,3,0,2,1:T(8,128)S(1)}, f32[2,1,1,8]{3,0,2,1:T(2,128)S(1)}, f32[2,1,1,8]{3,0,2,1:T(2,128)S(1)}, f32[2,1,1,8,128]{...) while((s32[]{:T(128)}, f32[2,1,1,8,128]{4,3,0,2,1:T(8,128)S(1)}, ...), condition=%wide.region_7.8_spmd, body=%wide.region_4.7_spmd.sunk | while | flops 12609602 | bytes 943761 | solution.py:89
  10.9 4.7 collective-permute-start
  31.7 4.5 collective-permute-start.1
  59.8 4.0 collective-permute-start.1
  73.5 4.1 collective-permute-start.1
  87.8 5.0 collective-permute-start.1
  102.4 4.7 collective-permute-start.1
  116.7 4.7 collective-permute-start.1
  131.1 4.0 collective-permute-start.1
  144.7 4.3 collective-permute-start.1
  158.7 4.0 collective-permute-start.1
  172.3 4.6 collective-permute-start.1
  186.6 4.7 collective-permute-start.1
  200.9 4.7 collective-permute-start.1
  215.2 4.7 collective-permute-start.1
  229.5 4.7 collective-permute-start.1
  243.8 4.0 collective-permute-start.1
  257.5 4.0 collective-permute-start.1
  271.2 4.0 collective-permute-start.1
  284.9 4.0 collective-permute-start.1
  298.5 4.0 collective-permute-start.1
  312.2 4.0 collective-permute-start.1
  325.9 4.0 collective-permute-start.1
  339.6 4.0 collective-permute-start.1
  353.2 4.0 collective-permute-start.1
  366.9 4.0 collective-permute-start.1
  380.6 4.0 collective-permute-start.1
  394.2 4.0 collective-permute-start.1
  407.9 4.0 collective-permute-start.1
  421.6 4.0 collective-permute-start.1
  435.3 4.0 collective-permute-start.1
  448.9 4.0 collective-permute-start.1
  462.6 4.0 collective-permute-start.1
  476.3 4.0 collective-permute-start.1
  490.0 4.0 collective-permute-start.1
  503.6 4.0 collective-permute-start.1
  517.3 4.0 collective-permute-start.1
  531.0 4.0 collective-permute-start.1
  544.6 4.0 collective-permute-start.1
  558.3 4.0 collective-permute-start.1
  572.0 4.0 collective-permute-start.1
  585.7 4.0 collective-permute-start.1
  599.3 4.0 collective-permute-start.1
  613.0 4.0 collective-permute-start.1
  626.7 4.0 collective-permute-start.1
  640.4 4.0 collective-permute-start.1
  893.6 64.9 %all_gather.3 = f32[2,64,1024]{2,0,1:T(2,128)S(1)} all-gather(f32[2,1,1024]{2,0,1:T(2,128)S(1)} %reshape.143), channel_id=1, replica_groups=mesh['ctx'=64,'head'=8] {'ctx'}, dimensions={1}, use_global_device_ids=true | all-gather | bytes 532480 | tf_op jit(solution)/shard_map/all_gather | solution.py:97
  959.9 72.6 %reduce-scatter.2.cloned.1.call-done = f32[2,8,80]{2,1,0:T(8,128)} async-done(((f32[2,64,80]{2,1,0:T(8,128)}), f32[2,8,80]{2,1,0:T(8,128)}) %reduce-scatter.2.cloned.1.call-update) | async-done | bytes 5136 | tf_op jit(solution)/shard_map/reduce_scatter | solution.py:101
  (940 shorter events, 694.4 us)
Async XLA Ops:
  6.5 1026.0 %reduce-scatter.2.cloned.1.call-start = ((), (), s32[]{:S(2)}) async-start(), calls=%async_computation.1 | async-start | bytes 73728 | tf_op jit(solution)/shard_map/reduce_scatter | solution.py:101
  10.9 16.1 %collective-permute-start = (f32[2,1,1,8,128]{4,3,0,2,1:T(8,128)S(1)}, f32[2,1,1,8,128]{4,3,0,2,1:T(8,128)S(1)}, u32[]{:S(2)}, u32[]{:S(2)}) collective-permute-start(f32[2,1,1,8,128]{4,3,0,2,1:T(8,128)S(1)} %copy.39), channel_id=1, source_target_pairs={{0,8},{8,16},{16,24},{24,32},{32,40},{40,48},{48,56},{56,64},{64,7... | collective-permute-start | bytes 24584 | tf_op jit(solution)/shard_map/while/body/eval_jaxpr/ppermute | solution.py:12
  27.0 14.4 %collective-permute-start = (f32[2,1,1,8,128]{4,3,0,2,1:T(8,128)S(1)}, f32[2,1,1,8,128]{4,3,0,2,1:T(8,128)S(1)}, u32[]{:S(2)}, u32[]{:S(2)}) collective-permute-start(f32[2,1,1,8,128]{4,3,0,2,1:T(8,128)S(1)} %copy.39), channel_id=1, source_target_pairs={{0,8},{8,16},{16,24},{24,32},{32,40},{40,48},{48,56},{56,64},{64,7... | collective-permute-start | bytes 24584 | tf_op jit(solution)/shard_map/while/body/eval_jaxpr/ppermute | solution.py:12
  41.4 13.7 %collective-permute-start = (f32[2,1,1,8,128]{4,3,0,2,1:T(8,128)S(1)}, f32[2,1,1,8,128]{4,3,0,2,1:T(8,128)S(1)}, u32[]{:S(2)}, u32[]{:S(2)}) collective-permute-start(f32[2,1,1,8,128]{4,3,0,2,1:T(8,128)S(1)} %copy.39), channel_id=1, source_target_pairs={{0,8},{8,16},{16,24},{24,32},{32,40},{40,48},{48,56},{56,64},{64,7... | collective-permute-start | bytes 24584 | tf_op jit(solution)/shard_map/while/body/eval_jaxpr/ppermute | solution.py:12
  55.1 13.7 %collective-permute-start = (f32[2,1,1,8,128]{4,3,0,2,1:T(8,128)S(1)}, f32[2,1,1,8,128]{4,3,0,2,1:T(8,128)S(1)}, u32[]{:S(2)}, u32[]{:S(2)}) collective-permute-start(f32[2,1,1,8,128]{4,3,0,2,1:T(8,128)S(1)} %copy.39), channel_id=1, source_target_pairs={{0,8},{8,16},{16,24},{24,32},{32,40},{40,48},{48,56},{56,64},{64,7... | collective-permute-start | bytes 24584 | tf_op jit(solution)/shard_map/while/body/eval_jaxpr/ppermute | solution.py:12
  68.7 13.7 %collective-permute-start = (f32[2,1,1,8,128]{4,3,0,2,1:T(8,128)S(1)}, f32[2,1,1,8,128]{4,3,0,2,1:T(8,128)S(1)}, u32[]{:S(2)}, u32[]{:S(2)}) collective-permute-start(f32[2,1,1,8,128]{4,3,0,2,1:T(8,128)S(1)} %copy.39), channel_id=1, source_target_pairs={{0,8},{8,16},{16,24},{24,32},{32,40},{40,48},{48,56},{56,64},{64,7... | collective-permute-start | bytes 24584 | tf_op jit(solution)/shard_map/while/body/eval_jaxpr/ppermute | solution.py:12
  82.4 13.7 %collective-permute-start = (f32[2,1,1,8,128]{4,3,0,2,1:T(8,128)S(1)}, f32[2,1,1,8,128]{4,3,0,2,1:T(8,128)S(1)}, u32[]{:S(2)}, u32[]{:S(2)}) collective-permute-start(f32[2,1,1,8,128]{4,3,0,2,1:T(8,128)S(1)} %copy.39), channel_id=1, source_target_pairs={{0,8},{8,16},{16,24},{24,32},{32,40},{40,48},{48,56},{56,64},{64,7... | collective-permute-start | bytes 24584 | tf_op jit(solution)/shard_map/while/body/eval_jaxpr/ppermute | solution.py:12
  96.1 14.1 %collective-permute-start = (f32[2,1,1,8,128]{4,3,0,2,1:T(8,128)S(1)}, f32[2,1,1,8,128]{4,3,0,2,1:T(8,128)S(1)}, u32[]{:S(2)}, u32[]{:S(2)}) collective-permute-start(f32[2,1,1,8,128]{4,3,0,2,1:T(8,128)S(1)} %copy.39), channel_id=1, source_target_pairs={{0,8},{8,16},{16,24},{24,32},{32,40},{40,48},{48,56},{56,64},{64,7... | collective-permute-start | bytes 24584 | tf_op jit(solution)/shard_map/while/body/eval_jaxpr/ppermute | solution.py:12
  110.2 14.3 %collective-permute-start = (f32[2,1,1,8,128]{4,3,0,2,1:T(8,128)S(1)}, f32[2,1,1,8,128]{4,3,0,2,1:T(8,128)S(1)}, u32[]{:S(2)}, u32[]{:S(2)}) collective-permute-start(f32[2,1,1,8,128]{4,3,0,2,1:T(8,128)S(1)} %copy.39), channel_id=1, source_target_pairs={{0,8},{8,16},{16,24},{24,32},{32,40},{40,48},{48,56},{56,64},{64,7... | collective-permute-start | bytes 24584 | tf_op jit(solution)/shard_map/while/body/eval_jaxpr/ppermute | solution.py:12
  124.5 13.7 %collective-permute-start = (f32[2,1,1,8,128]{4,3,0,2,1:T(8,128)S(1)}, f32[2,1,1,8,128]{4,3,0,2,1:T(8,128)S(1)}, u32[]{:S(2)}, u32[]{:S(2)}) collective-permute-start(f32[2,1,1,8,128]{4,3,0,2,1:T(8,128)S(1)} %copy.39), channel_id=1, source_target_pairs={{0,8},{8,16},{16,24},{24,32},{32,40},{40,48},{48,56},{56,64},{64,7... | collective-permute-start | bytes 24584 | tf_op jit(solution)/shard_map/while/body/eval_jaxpr/ppermute | solution.py:12
  138.2 13.9 %collective-permute-start = (f32[2,1,1,8,128]{4,3,0,2,1:T(8,128)S(1)}, f32[2,1,1,8,128]{4,3,0,2,1:T(8,128)S(1)}, u32[]{:S(2)}, u32[]{:S(2)}) collective-permute-start(f32[2,1,1,8,128]{4,3,0,2,1:T(8,128)S(1)} %copy.39), channel_id=1, source_target_pairs={{0,8},{8,16},{16,24},{24,32},{32,40},{40,48},{48,56},{56,64},{64,7... | collective-permute-start | bytes 24584 | tf_op jit(solution)/shard_map/while/body/eval_jaxpr/ppermute | solution.py:12
  152.1 13.7 %collective-permute-start = (f32[2,1,1,8,128]{4,3,0,2,1:T(8,128)S(1)}, f32[2,1,1,8,128]{4,3,0,2,1:T(8,128)S(1)}, u32[]{:S(2)}, u32[]{:S(2)}) collective-permute-start(f32[2,1,1,8,128]{4,3,0,2,1:T(8,128)S(1)} %copy.39), channel_id=1, source_target_pairs={{0,8},{8,16},{16,24},{24,32},{32,40},{40,48},{48,56},{56,64},{64,7... | collective-permute-start | bytes 24584 | tf_op jit(solution)/shard_map/while/body/eval_jaxpr/ppermute | solution.py:12
  165.7 14.2 %collective-permute-start = (f32[2,1,1,8,128]{4,3,0,2,1:T(8,128)S(1)}, f32[2,1,1,8,128]{4,3,0,2,1:T(8,128)S(1)}, u32[]{:S(2)}, u32[]{:S(2)}) collective-permute-start(f32[2,1,1,8,128]{4,3,0,2,1:T(8,128)S(1)} %copy.39), channel_id=1, source_target_pairs={{0,8},{8,16},{16,24},{24,32},{32,40},{40,48},{48,56},{56,64},{64,7... | collective-permute-start | bytes 24584 | tf_op jit(solution)/shard_map/while/body/eval_jaxpr/ppermute | solution.py:12
  180.0 14.3 %collective-permute-start = (f32[2,1,1,8,128]{4,3,0,2,1:T(8,128)S(1)}, f32[2,1,1,8,128]{4,3,0,2,1:T(8,128)S(1)}, u32[]{:S(2)}, u32[]{:S(2)}) collective-permute-start(f32[2,1,1,8,128]{4,3,0,2,1:T(8,128)S(1)} %copy.39), channel_id=1, source_target_pairs={{0,8},{8,16},{16,24},{24,32},{32,40},{40,48},{48,56},{56,64},{64,7... | collective-permute-start | bytes 24584 | tf_op jit(solution)/shard_map/while/body/eval_jaxpr/ppermute | solution.py:12
  194.3 14.3 %collective-permute-start = (f32[2,1,1,8,128]{4,3,0,2,1:T(8,128)S(1)}, f32[2,1,1,8,128]{4,3,0,2,1:T(8,128)S(1)}, u32[]{:S(2)}, u32[]{:S(2)}) collective-permute-start(f32[2,1,1,8,128]{4,3,0,2,1:T(8,128)S(1)} %copy.39), channel_id=1, source_target_pairs={{0,8},{8,16},{16,24},{24,32},{32,40},{40,48},{48,56},{56,64},{64,7... | collective-permute-start | bytes 24584 | tf_op jit(solution)/shard_map/while/body/eval_jaxpr/ppermute | solution.py:12
  208.6 14.3 %collective-permute-start = (f32[2,1,1,8,128]{4,3,0,2,1:T(8,128)S(1)}, f32[2,1,1,8,128]{4,3,0,2,1:T(8,128)S(1)}, u32[]{:S(2)}, u32[]{:S(2)}) collective-permute-start(f32[2,1,1,8,128]{4,3,0,2,1:T(8,128)S(1)} %copy.39), channel_id=1, source_target_pairs={{0,8},{8,16},{16,24},{24,32},{32,40},{40,48},{48,56},{56,64},{64,7... | collective-permute-start | bytes 24584 | tf_op jit(solution)/shard_map/while/body/eval_jaxpr/ppermute | solution.py:12
  222.9 14.3 %collective-permute-start = (f32[2,1,1,8,128]{4,3,0,2,1:T(8,128)S(1)}, f32[2,1,1,8,128]{4,3,0,2,1:T(8,128)S(1)}, u32[]{:S(2)}, u32[]{:S(2)}) collective-permute-start(f32[2,1,1,8,128]{4,3,0,2,1:T(8,128)S(1)} %copy.39), channel_id=1, source_target_pairs={{0,8},{8,16},{16,24},{24,32},{32,40},{40,48},{48,56},{56,64},{64,7... | collective-permute-start | bytes 24584 | tf_op jit(solution)/shard_map/while/body/eval_jaxpr/ppermute | solution.py:12
  237.3 13.7 %collective-permute-start = (f32[2,1,1,8,128]{4,3,0,2,1:T(8,128)S(1)}, f32[2,1,1,8,128]{4,3,0,2,1:T(8,128)S(1)}, u32[]{:S(2)}, u32[]{:S(2)}) collective-permute-start(f32[2,1,1,8,128]{4,3,0,2,1:T(8,128)S(1)} %copy.39), channel_id=1, source_target_pairs={{0,8},{8,16},{16,24},{24,32},{32,40},{40,48},{48,56},{56,64},{64,7... | collective-permute-start | bytes 24584 | tf_op jit(solution)/shard_map/while/body/eval_jaxpr/ppermute | solution.py:12
  250.9 13.7 %collective-permute-start = (f32[2,1,1,8,128]{4,3,0,2,1:T(8,128)S(1)}, f32[2,1,1,8,128]{4,3,0,2,1:T(8,128)S(1)}, u32[]{:S(2)}, u32[]{:S(2)}) collective-permute-start(f32[2,1,1,8,128]{4,3,0,2,1:T(8,128)S(1)} %copy.39), channel_id=1, source_target_pairs={{0,8},{8,16},{16,24},{24,32},{32,40},{40,48},{48,56},{56,64},{64,7... | collective-permute-start | bytes 24584 | tf_op jit(solution)/shard_map/while/body/eval_jaxpr/ppermute | solution.py:12
  264.6 13.7 %collective-permute-start = (f32[2,1,1,8,128]{4,3,0,2,1:T(8,128)S(1)}, f32[2,1,1,8,128]{4,3,0,2,1:T(8,128)S(1)}, u32[]{:S(2)}, u32[]{:S(2)}) collective-permute-start(f32[2,1,1,8,128]{4,3,0,2,1:T(8,128)S(1)} %copy.39), channel_id=1, source_target_pairs={{0,8},{8,16},{16,24},{24,32},{32,40},{40,48},{48,56},{56,64},{64,7... | collective-permute-start | bytes 24584 | tf_op jit(solution)/shard_map/while/body/eval_jaxpr/ppermute | solution.py:12
  278.3 13.7 %collective-permute-start = (f32[2,1,1,8,128]{4,3,0,2,1:T(8,128)S(1)}, f32[2,1,1,8,128]{4,3,0,2,1:T(8,128)S(1)}, u32[]{:S(2)}, u32[]{:S(2)}) collective-permute-start(f32[2,1,1,8,128]{4,3,0,2,1:T(8,128)S(1)} %copy.39), channel_id=1, source_target_pairs={{0,8},{8,16},{16,24},{24,32},{32,40},{40,48},{48,56},{56,64},{64,7... | collective-permute-start | bytes 24584 | tf_op jit(solution)/shard_map/while/body/eval_jaxpr/ppermute | solution.py:12
  292.0 13.7 %collective-permute-start = (f32[2,1,1,8,128]{4,3,0,2,1:T(8,128)S(1)}, f32[2,1,1,8,128]{4,3,0,2,1:T(8,128)S(1)}, u32[]{:S(2)}, u32[]{:S(2)}) collective-permute-start(f32[2,1,1,8,128]{4,3,0,2,1:T(8,128)S(1)} %copy.39), channel_id=1, source_target_pairs={{0,8},{8,16},{16,24},{24,32},{32,40},{40,48},{48,56},{56,64},{64,7... | collective-permute-start | bytes 24584 | tf_op jit(solution)/shard_map/while/body/eval_jaxpr/ppermute | solution.py:12
  305.6 13.7 %collective-permute-start = (f32[2,1,1,8,128]{4,3,0,2,1:T(8,128)S(1)}, f32[2,1,1,8,128]{4,3,0,2,1:T(8,128)S(1)}, u32[]{:S(2)}, u32[]{:S(2)}) collective-permute-start(f32[2,1,1,8,128]{4,3,0,2,1:T(8,128)S(1)} %copy.39), channel_id=1, source_target_pairs={{0,8},{8,16},{16,24},{24,32},{32,40},{40,48},{48,56},{56,64},{64,7... | collective-permute-start | bytes 24584 | tf_op jit(solution)/shard_map/while/body/eval_jaxpr/ppermute | solution.py:12
  319.3 13.7 %collective-permute-start = (f32[2,1,1,8,128]{4,3,0,2,1:T(8,128)S(1)}, f32[2,1,1,8,128]{4,3,0,2,1:T(8,128)S(1)}, u32[]{:S(2)}, u32[]{:S(2)}) collective-permute-start(f32[2,1,1,8,128]{4,3,0,2,1:T(8,128)S(1)} %copy.39), channel_id=1, source_target_pairs={{0,8},{8,16},{16,24},{24,32},{32,40},{40,48},{48,56},{56,64},{64,7... | collective-permute-start | bytes 24584 | tf_op jit(solution)/shard_map/while/body/eval_jaxpr/ppermute | solution.py:12
  333.0 13.7 %collective-permute-start = (f32[2,1,1,8,128]{4,3,0,2,1:T(8,128)S(1)}, f32[2,1,1,8,128]{4,3,0,2,1:T(8,128)S(1)}, u32[]{:S(2)}, u32[]{:S(2)}) collective-permute-start(f32[2,1,1,8,128]{4,3,0,2,1:T(8,128)S(1)} %copy.39), channel_id=1, source_target_pairs={{0,8},{8,16},{16,24},{24,32},{32,40},{40,48},{48,56},{56,64},{64,7... | collective-permute-start | bytes 24584 | tf_op jit(solution)/shard_map/while/body/eval_jaxpr/ppermute | solution.py:12
  346.6 13.7 %collective-permute-start = (f32[2,1,1,8,128]{4,3,0,2,1:T(8,128)S(1)}, f32[2,1,1,8,128]{4,3,0,2,1:T(8,128)S(1)}, u32[]{:S(2)}, u32[]{:S(2)}) collective-permute-start(f32[2,1,1,8,128]{4,3,0,2,1:T(8,128)S(1)} %copy.39), channel_id=1, source_target_pairs={{0,8},{8,16},{16,24},{24,32},{32,40},{40,48},{48,56},{56,64},{64,7... | collective-permute-start | bytes 24584 | tf_op jit(solution)/shard_map/while/body/eval_jaxpr/ppermute | solution.py:12
  360.3 13.7 %collective-permute-start = (f32[2,1,1,8,128]{4,3,0,2,1:T(8,128)S(1)}, f32[2,1,1,8,128]{4,3,0,2,1:T(8,128)S(1)}, u32[]{:S(2)}, u32[]{:S(2)}) collective-permute-start(f32[2,1,1,8,128]{4,3,0,2,1:T(8,128)S(1)} %copy.39), channel_id=1, source_target_pairs={{0,8},{8,16},{16,24},{24,32},{32,40},{40,48},{48,56},{56,64},{64,7... | collective-permute-start | bytes 24584 | tf_op jit(solution)/shard_map/while/body/eval_jaxpr/ppermute | solution.py:12
  374.0 13.7 %collective-permute-start = (f32[2,1,1,8,128]{4,3,0,2,1:T(8,128)S(1)}, f32[2,1,1,8,128]{4,3,0,2,1:T(8,128)S(1)}, u32[]{:S(2)}, u32[]{:S(2)}) collective-permute-start(f32[2,1,1,8,128]{4,3,0,2,1:T(8,128)S(1)} %copy.39), channel_id=1, source_target_pairs={{0,8},{8,16},{16,24},{24,32},{32,40},{40,48},{48,56},{56,64},{64,7... | collective-permute-start | bytes 24584 | tf_op jit(solution)/shard_map/while/body/eval_jaxpr/ppermute | solution.py:12
  387.7 13.7 %collective-permute-start = (f32[2,1,1,8,128]{4,3,0,2,1:T(8,128)S(1)}, f32[2,1,1,8,128]{4,3,0,2,1:T(8,128)S(1)}, u32[]{:S(2)}, u32[]{:S(2)}) collective-permute-start(f32[2,1,1,8,128]{4,3,0,2,1:T(8,128)S(1)} %copy.39), channel_id=1, source_target_pairs={{0,8},{8,16},{16,24},{24,32},{32,40},{40,48},{48,56},{56,64},{64,7... | collective-permute-start | bytes 24584 | tf_op jit(solution)/shard_map/while/body/eval_jaxpr/ppermute | solution.py:12
  401.3 13.7 %collective-permute-start = (f32[2,1,1,8,128]{4,3,0,2,1:T(8,128)S(1)}, f32[2,1,1,8,128]{4,3,0,2,1:T(8,128)S(1)}, u32[]{:S(2)}, u32[]{:S(2)}) collective-permute-start(f32[2,1,1,8,128]{4,3,0,2,1:T(8,128)S(1)} %copy.39), channel_id=1, source_target_pairs={{0,8},{8,16},{16,24},{24,32},{32,40},{40,48},{48,56},{56,64},{64,7... | collective-permute-start | bytes 24584 | tf_op jit(solution)/shard_map/while/body/eval_jaxpr/ppermute | solution.py:12
  415.0 13.7 %collective-permute-start = (f32[2,1,1,8,128]{4,3,0,2,1:T(8,128)S(1)}, f32[2,1,1,8,128]{4,3,0,2,1:T(8,128)S(1)}, u32[]{:S(2)}, u32[]{:S(2)}) collective-permute-start(f32[2,1,1,8,128]{4,3,0,2,1:T(8,128)S(1)} %copy.39), channel_id=1, source_target_pairs={{0,8},{8,16},{16,24},{24,32},{32,40},{40,48},{48,56},{56,64},{64,7... | collective-permute-start | bytes 24584 | tf_op jit(solution)/shard_map/while/body/eval_jaxpr/ppermute | solution.py:12
  469.7 13.7 %collective-permute-start = (f32[2,1,1,8,128]{4,3,0,2,1:T(8,128)S(1)}, f32[2,1,1,8,128]{4,3,0,2,1:T(8,128)S(1)}, u32[]{:S(2)}, u32[]{:S(2)}) collective-permute-start(f32[2,1,1,8,128]{4,3,0,2,1:T(8,128)S(1)} %copy.39), channel_id=1, source_target_pairs={{0,8},{8,16},{16,24},{24,32},{32,40},{40,48},{48,56},{56,64},{64,7... | collective-permute-start | bytes 24584 | tf_op jit(solution)/shard_map/while/body/eval_jaxpr/ppermute | solution.py:12
  483.4 13.7 %collective-permute-start = (f32[2,1,1,8,128]{4,3,0,2,1:T(8,128)S(1)}, f32[2,1,1,8,128]{4,3,0,2,1:T(8,128)S(1)}, u32[]{:S(2)}, u32[]{:S(2)}) collective-permute-start(f32[2,1,1,8,128]{4,3,0,2,1:T(8,128)S(1)} %copy.39), channel_id=1, source_target_pairs={{0,8},{8,16},{16,24},{24,32},{32,40},{40,48},{48,56},{56,64},{64,7... | collective-permute-start | bytes 24584 | tf_op jit(solution)/shard_map/while/body/eval_jaxpr/ppermute | solution.py:12
  497.0 13.7 %collective-permute-start = (f32[2,1,1,8,128]{4,3,0,2,1:T(8,128)S(1)}, f32[2,1,1,8,128]{4,3,0,2,1:T(8,128)S(1)}, u32[]{:S(2)}, u32[]{:S(2)}) collective-permute-start(f32[2,1,1,8,128]{4,3,0,2,1:T(8,128)S(1)} %copy.39), channel_id=1, source_target_pairs={{0,8},{8,16},{16,24},{24,32},{32,40},{40,48},{48,56},{56,64},{64,7... | collective-permute-start | bytes 24584 | tf_op jit(solution)/shard_map/while/body/eval_jaxpr/ppermute | solution.py:12
  510.7 13.7 %collective-permute-start = (f32[2,1,1,8,128]{4,3,0,2,1:T(8,128)S(1)}, f32[2,1,1,8,128]{4,3,0,2,1:T(8,128)S(1)}, u32[]{:S(2)}, u32[]{:S(2)}) collective-permute-start(f32[2,1,1,8,128]{4,3,0,2,1:T(8,128)S(1)} %copy.39), channel_id=1, source_target_pairs={{0,8},{8,16},{16,24},{24,32},{32,40},{40,48},{48,56},{56,64},{64,7... | collective-permute-start | bytes 24584 | tf_op jit(solution)/shard_map/while/body/eval_jaxpr/ppermute | solution.py:12
  524.4 13.7 %collective-permute-start = (f32[2,1,1,8,128]{4,3,0,2,1:T(8,128)S(1)}, f32[2,1,1,8,128]{4,3,0,2,1:T(8,128)S(1)}, u32[]{:S(2)}, u32[]{:S(2)}) collective-permute-start(f32[2,1,1,8,128]{4,3,0,2,1:T(8,128)S(1)} %copy.39), channel_id=1, source_target_pairs={{0,8},{8,16},{16,24},{24,32},{32,40},{40,48},{48,56},{56,64},{64,7... | collective-permute-start | bytes 24584 | tf_op jit(solution)/shard_map/while/body/eval_jaxpr/ppermute | solution.py:12
  606.4 13.7 %collective-permute-start = (f32[2,1,1,8,128]{4,3,0,2,1:T(8,128)S(1)}, f32[2,1,1,8,128]{4,3,0,2,1:T(8,128)S(1)}, u32[]{:S(2)}, u32[]{:S(2)}) collective-permute-start(f32[2,1,1,8,128]{4,3,0,2,1:T(8,128)S(1)} %copy.39), channel_id=1, source_target_pairs={{0,8},{8,16},{16,24},{24,32},{32,40},{40,48},{48,56},{56,64},{64,7... | collective-permute-start | bytes 24584 | tf_op jit(solution)/shard_map/while/body/eval_jaxpr/ppermute | solution.py:12
  620.1 13.7 %collective-permute-start = (f32[2,1,1,8,128]{4,3,0,2,1:T(8,128)S(1)}, f32[2,1,1,8,128]{4,3,0,2,1:T(8,128)S(1)}, u32[]{:S(2)}, u32[]{:S(2)}) collective-permute-start(f32[2,1,1,8,128]{4,3,0,2,1:T(8,128)S(1)} %copy.39), channel_id=1, source_target_pairs={{0,8},{8,16},{16,24},{24,32},{32,40},{40,48},{48,56},{56,64},{64,7... | collective-permute-start | bytes 24584 | tf_op jit(solution)/shard_map/while/body/eval_jaxpr/ppermute | solution.py:12
  633.8 13.7 %collective-permute-start = (f32[2,1,1,8,128]{4,3,0,2,1:T(8,128)S(1)}, f32[2,1,1,8,128]{4,3,0,2,1:T(8,128)S(1)}, u32[]{:S(2)}, u32[]{:S(2)}) collective-permute-start(f32[2,1,1,8,128]{4,3,0,2,1:T(8,128)S(1)} %copy.39), channel_id=1, source_target_pairs={{0,8},{8,16},{16,24},{24,32},{32,40},{40,48},{48,56},{56,64},{64,7... | collective-permute-start | bytes 24584 | tf_op jit(solution)/shard_map/while/body/eval_jaxpr/ppermute | solution.py:12
  647.5 13.7 %collective-permute-start = (f32[2,1,1,8,128]{4,3,0,2,1:T(8,128)S(1)}, f32[2,1,1,8,128]{4,3,0,2,1:T(8,128)S(1)}, u32[]{:S(2)}, u32[]{:S(2)}) collective-permute-start(f32[2,1,1,8,128]{4,3,0,2,1:T(8,128)S(1)} %copy.39), channel_id=1, source_target_pairs={{0,8},{8,16},{16,24},{24,32},{32,40},{40,48},{48,56},{56,64},{64,7... | collective-permute-start | bytes 24584 | tf_op jit(solution)/shard_map/while/body/eval_jaxpr/ppermute | solution.py:12
  661.1 13.7 %collective-permute-start = (f32[2,1,1,8,128]{4,3,0,2,1:T(8,128)S(1)}, f32[2,1,1,8,128]{4,3,0,2,1:T(8,128)S(1)}, u32[]{:S(2)}, u32[]{:S(2)}) collective-permute-start(f32[2,1,1,8,128]{4,3,0,2,1:T(8,128)S(1)} %copy.39), channel_id=1, source_target_pairs={{0,8},{8,16},{16,24},{24,32},{32,40},{40,48},{48,56},{56,64},{64,7... | collective-permute-start | bytes 24584 | tf_op jit(solution)/shard_map/while/body/eval_jaxpr/ppermute | solution.py:12
  729.5 13.7 %collective-permute-start = (f32[2,1,1,8,128]{4,3,0,2,1:T(8,128)S(1)}, f32[2,1,1,8,128]{4,3,0,2,1:T(8,128)S(1)}, u32[]{:S(2)}, u32[]{:S(2)}) collective-permute-start(f32[2,1,1,8,128]{4,3,0,2,1:T(8,128)S(1)} %copy.39), channel_id=1, source_target_pairs={{0,8},{8,16},{16,24},{24,32},{32,40},{40,48},{48,56},{56,64},{64,7... | collective-permute-start | bytes 24584 | tf_op jit(solution)/shard_map/while/body/eval_jaxpr/ppermute | solution.py:12
  743.2 13.7 %collective-permute-start = (f32[2,1,1,8,128]{4,3,0,2,1:T(8,128)S(1)}, f32[2,1,1,8,128]{4,3,0,2,1:T(8,128)S(1)}, u32[]{:S(2)}, u32[]{:S(2)}) collective-permute-start(f32[2,1,1,8,128]{4,3,0,2,1:T(8,128)S(1)} %copy.39), channel_id=1, source_target_pairs={{0,8},{8,16},{16,24},{24,32},{32,40},{40,48},{48,56},{56,64},{64,7... | collective-permute-start | bytes 24584 | tf_op jit(solution)/shard_map/while/body/eval_jaxpr/ppermute | solution.py:12
  756.8 13.7 %collective-permute-start = (f32[2,1,1,8,128]{4,3,0,2,1:T(8,128)S(1)}, f32[2,1,1,8,128]{4,3,0,2,1:T(8,128)S(1)}, u32[]{:S(2)}, u32[]{:S(2)}) collective-permute-start(f32[2,1,1,8,128]{4,3,0,2,1:T(8,128)S(1)} %copy.39), channel_id=1, source_target_pairs={{0,8},{8,16},{16,24},{24,32},{32,40},{40,48},{48,56},{56,64},{64,7... | collective-permute-start | bytes 24584 | tf_op jit(solution)/shard_map/while/body/eval_jaxpr/ppermute | solution.py:12
  770.5 13.7 %collective-permute-start = (f32[2,1,1,8,128]{4,3,0,2,1:T(8,128)S(1)}, f32[2,1,1,8,128]{4,3,0,2,1:T(8,128)S(1)}, u32[]{:S(2)}, u32[]{:S(2)}) collective-permute-start(f32[2,1,1,8,128]{4,3,0,2,1:T(8,128)S(1)} %copy.39), channel_id=1, source_target_pairs={{0,8},{8,16},{16,24},{24,32},{32,40},{40,48},{48,56},{56,64},{64,7... | collective-permute-start | bytes 24584 | tf_op jit(solution)/shard_map/while/body/eval_jaxpr/ppermute | solution.py:12
  784.2 13.7 %collective-permute-start = (f32[2,1,1,8,128]{4,3,0,2,1:T(8,128)S(1)}, f32[2,1,1,8,128]{4,3,0,2,1:T(8,128)S(1)}, u32[]{:S(2)}, u32[]{:S(2)}) collective-permute-start(f32[2,1,1,8,128]{4,3,0,2,1:T(8,128)S(1)} %copy.39), channel_id=1, source_target_pairs={{0,8},{8,16},{16,24},{24,32},{32,40},{40,48},{48,56},{56,64},{64,7... | collective-permute-start | bytes 24584 | tf_op jit(solution)/shard_map/while/body/eval_jaxpr/ppermute | solution.py:12
  866.2 13.7 %collective-permute-start = (f32[2,1,1,8,128]{4,3,0,2,1:T(8,128)S(1)}, f32[2,1,1,8,128]{4,3,0,2,1:T(8,128)S(1)}, u32[]{:S(2)}, u32[]{:S(2)}) collective-permute-start(f32[2,1,1,8,128]{4,3,0,2,1:T(8,128)S(1)} %copy.39), channel_id=1, source_target_pairs={{0,8},{8,16},{16,24},{24,32},{32,40},{40,48},{48,56},{56,64},{64,7... | collective-permute-start | bytes 24584 | tf_op jit(solution)/shard_map/while/body/eval_jaxpr/ppermute | solution.py:12
  879.9 13.7 %collective-permute-start = (f32[2,1,1,8,128]{4,3,0,2,1:T(8,128)S(1)}, f32[2,1,1,8,128]{4,3,0,2,1:T(8,128)S(1)}, u32[]{:S(2)}, u32[]{:S(2)}) collective-permute-start(f32[2,1,1,8,128]{4,3,0,2,1:T(8,128)S(1)} %copy.39), channel_id=1, source_target_pairs={{0,8},{8,16},{16,24},{24,32},{32,40},{40,48},{48,56},{56,64},{64,7... | collective-permute-start | bytes 24584 | tf_op jit(solution)/shard_map/while/body/eval_jaxpr/ppermute | solution.py:12
  (277 other events, 2659.8 us)
Sparse Core Ops, SparseCore 0:
  960.0 72.4 reduce-scatter.1
where the time goes:
time: 1050 us; the launch traced here: 1040 us
  starting transfers between devices  752 us (72%)
  waiting for transfers between devices  153 us (15%)
  blocking collectives  64.9 us (6%)
  matrix products  36.6 us (3%)
  between operations  14.1 us (1%)
  other arithmetic  13.1 us (1%)
    ppermute x256, starting transfers between devices, from_behind(): return lax.ppermute(value, axis, pairs)  752 us
    ppermute x256, waiting for transfers between devices, from_behind(): return lax.ppermute(value, axis, pairs)  80.1 us
    reduce_scatter x1, waiting for transfers between devices, local(): lax.psum_scatter(partial_out, 'head', scatter_dimension=1, tiled=True)  72.6 us
    all_gather x1, blocking collectives, local(): lax.all_gather(attention, 'ctx', axis=1, tiled=True)  64.9 us
  transfers between devices with their start and end apart: 257, of which 70 were waited for; matrix products, arithmetic and copies ran while one was open for 4% of the time, Pallas kernels for 0%

commit v1 on v0

v1 whole, which is shorter than its diff:
```python
import jax
import jax.numpy as jnp
from jax import lax
from jax.experimental import pallas as pl
from jax.experimental.pallas import tpu as pltpu
from jax.sharding import PartitionSpec as P

MESH = pl.DeviceIdType.MESH
F32, BF16 = jnp.float32, jnp.bfloat16
Z, QUAD, HEADS = 16, 4, 8
WINDOW = 4
BLOCK = 16
HD = 128
NEAR = (12, 13, 14, 15, 0, 1, 2, 3)
FAR = (4, 5, 6, 7, 8, 9, 10, 11)
FAR_FIRST = sorted(range(1, Z), key=lambda d: -min(d, Z - d))


def nt(a, b):
    return lax.dot_general(a, b, (((1,), (1,)), ((), ())), preferred_element_type=F32)


def nn(a, b):
    return jnp.dot(a, b, preferred_element_type=F32)


def split2(x):
    high = x.astype(BF16)
    return high, (x - high.astype(F32)).astype(BF16)


def split3(x):
    high = x.astype(BF16)
    rest = x - high.astype(F32)
    middle = rest.astype(BF16)
    return high, middle, (rest - middle.astype(F32)).astype(BF16)


def kernel(
    q_in, k_in, v_in, sk_in, sv_in, nk_in, nv_in, len_in, w_in, out_ref,
    qbuf, kv, w, sk, sv, nk, nv, length, ka, kb, kc, vv, wh, wl,
    osend, orecv, lsend, lrecv, att, psend, precv,
    in_sem, a_send, a_recv, x_send, x_recv, o_send, o_recv, l_send, l_recv, c_send, c_recv, d_send, d_recv,
):
    ctx, head = lax.axis_index("ctx"), lax.axis_index("head")
    z, q = ctx // QUAD, lax.rem(ctx, QUAD)
    core, side = lax.rem(q, 2), q // 2

    def along(d):
        return (lax.rem(ctx + QUAD * (d % Z), Z * QUAD), head)

    def in_quad(k, d=0):
        c = 1 - core if k & 1 else core
        s = 1 - side if k & 2 else side
        return (z * QUAD + s * 2 + c, lax.rem(head + d, HEADS))

    def remote(src, dst, send, recv, to):
        return pltpu.make_async_remote_copy(
            src_ref=src, dst_ref=dst, send_sem=send, recv_sem=recv, device_id=to, device_id_type=MESH
        )

    window = [d for d in FAR_FIRST if min(d, Z - d) <= WINDOW]
    barrier = pltpu.get_barrier_semaphore()
    for d in window:
        pl.semaphore_signal(barrier, inc=1, device_id=along(d), device_id_type=MESH)
    mates = [(k, d) for d in (0, 2, 6, 4, 1, 3, 5, 7) for k in (2, 3, 1, 0) if (k, d) != (0, 0)]
    for k, d in mates:
        pl.semaphore_signal(barrier, inc=1, device_id=in_quad(k, d), device_id_type=MESH)

    own = [
        pltpu.make_async_copy(src, dst, in_sem.at[i])
        for i, (src, dst) in enumerate(
            (
                (q_in, qbuf.at[0]), (k_in, kv.at[0, 0]), (v_in, kv.at[0, 1]), (sk_in, sk), (sv_in, sv),
                (nk_in, nk), (nv_in, nv), (len_in, length), (w_in, w.at[0]),
            )
        )
    ]
    for c in own:
        c.start()
    pl.semaphore_wait(barrier, len(window) + len(mates))

    first = {d: remote(q_in, qbuf.at[Z - d], a_send.at[d], a_recv.at[d], along(d)) for d in window}
    for d in window:
        first[d].start()
    y_kv = [remote((k_in, v_in)[i], kv.at[2, i], x_send.at[i], x_recv.at[i], in_quad(2)) for i in (0, 1)]
    c_kv = [remote((k_in, v_in)[i], kv.at[1, i], x_send.at[2 + i], x_recv.at[2 + i], in_quad(1)) for i in (0, 1)]
    cy_kv = [remote(kv.at[2, i], kv.at[3, i], x_send.at[4 + i], x_recv.at[4 + i], in_quad(1)) for i in (0, 1)]
    y_w = remote(w_in, w.at[2], x_send.at[6], x_recv.at[6], in_quad(2))
    c_w = remote(w_in, w.at[1], x_send.at[7], x_recv.at[7], in_quad(1))
    cy_w = remote(w.at[2], w.at[3], x_send.at[8], x_recv.at[8], in_quad(1))
    for c in y_kv + c_kv:
        c.start()
    for c in own:
        c.wait()

    second = []
    for k in range(1, WINDOW + 1):
        first[Z - k].wait_recv()
        c = remote(qbuf.at[k], qbuf.at[k + WINDOW], a_send.at[Z + k], a_recv.at[Z + k], along(-WINDOW))
        c.start()
        second.append(c)
        first[k].wait_recv()
        if k < WINDOW:
            c = remote(
                qbuf.at[Z - k], qbuf.at[Z - k - WINDOW], a_send.at[Z + 8 + k], a_recv.at[Z + 8 + k], along(WINDOW)
            )
            c.start()
            second.append(c)

    def prepare(i):
        rows = pl.ds(i * 256, 256)
        high, middle, low = split3(kv[i, 0])
        ka[rows, :] = jnp.concatenate([high, high], axis=1)
        kb[rows, :] = jnp.concatenate([middle, middle], axis=1)
        kc[rows, :] = jnp.concatenate([low, high], axis=1)
        high, low = split2(kv[i, 1])
        vv[rows, :] = jnp.concatenate([high, low], axis=1)

    prepare(0)
    for c in c_kv:
        c.wait_recv()
    prepare(1)
    for i in (0, 1):
        y_kv[i].wait_recv()
        cy_kv[i].start()
    y_w.start()
    c_w.start()
    prepare(2)
    for c in cy_kv:
        c.wait_recv()
    prepare(3)

    scale = HD**-0.5
    lane = lax.broadcasted_iota(jnp.int32, (128, 128), 1)
    row = lax.broadcasted_iota(jnp.int32, (128, 128), 0)
    sends = []

    def prompt(b, slots):
        queries = jnp.concatenate([qbuf[s] for s in slots], axis=0)
        high, middle, low = split3(queries)
        qa = jnp.concatenate([high, middle], axis=1)
        qc = jnp.concatenate([high, low], axis=1)
        scores = nt(qa, ka[...]) + nt(qa, kb[...]) + nt(qc, kc[...])
        peak = jnp.max(scores, axis=1, keepdims=True)
        weights = jnp.exp((scores - peak) * scale)
        total = jnp.sum(weights, axis=1, keepdims=True)
        high, low = split2(weights)
        both = nn(high, vv[...]) + nn(low, vv[...])
        mixed = (both[:, :HD] + both[:, HD:]) / total
        logs = peak * scale + jnp.log(total)
        lsend[b] = jnp.sum(jnp.where(lane == row, logs, 0.0), axis=0, keepdims=True)
        for j, s in enumerate(slots):
            osend[s] = mixed[j * BLOCK : (j + 1) * BLOCK]
        for s in sorted(slots, key=lambda s: -min(s, Z - s)):
            if s:
                sends.append(remote(osend.at[s], orecv.at[Z - s], o_send.at[s], o_recv.at[s], along(s)))
                sends.append(remote(lsend.at[b], lrecv.at[Z - s], l_send.at[s], l_recv.at[s], along(s)))
                sends[-2].start()
                sends[-1].start()

    prompt(0, NEAR)
    for c in second:
        c.wait_recv()
    prompt(1, FAR)

    queries = qbuf[0]
    high, middle, low = split3(queries)
    kh, km, kl = split3(sk[...])
    scores = nt(high, kh) + nt(middle, kh) + nt(high, km) + nt(middle, km) + nt(high, kl) + nt(low, kh)
    lane16 = lax.broadcasted_iota(jnp.int32, (BLOCK, 128), 1)
    row16 = lax.broadcasted_iota(jnp.int32, (BLOCK, 128), 0)
    scores = jnp.where(lane16 < length[0], scores * scale, -1e30)
    fresh = nk[...]
    new0 = jnp.sum(queries * fresh[0:1], axis=1, keepdims=True) * scale
    new1 = jnp.sum(queries * fresh[1:2], axis=1, keepdims=True) * scale
    new1 = jnp.where(row16[:, :1] >= 8, new1, -1e30)
    peak = jnp.maximum(jnp.max(scores, axis=1, keepdims=True), jnp.maximum(new0, new1))
    weights, new0, new1 = jnp.exp(scores - peak), jnp.exp(new0 - peak), jnp.exp(new1 - peak)
    total = jnp.sum(weights, axis=1, keepdims=True) + new0 + new1
    wth, wtl = split2(weights)
    vh, vl = split2(sv[...])
    fresh = nv[...]
    mixed = nn(wth, vh) + nn(wth, vl) + nn(wtl, vh) + new0 * fresh[0:1] + new1 * fresh[1:2]
    parts = [(peak + jnp.log(total), mixed / total)]

    def columns(k):
        high, low = split2(w[k])
        wh[k, 0:80] = high
        wl[k, 0:80] = low
        wh[k, 80:128] = jnp.zeros((48, 1024), BF16)
        wl[k, 80:128] = jnp.zeros((48, 1024), BF16)

    columns(0)
    c_w.wait_recv()
    columns(1)
    y_w.wait_recv()
    cy_w.start()
    columns(2)
    cy_w.wait_recv()
    columns(3)

    def logs_of(values, j):
        return jnp.sum(jnp.where(lane16 == row16 + BLOCK * j, values, 0.0), axis=1, keepdims=True)

    parts.append((logs_of(lsend[0], NEAR.index(0)), osend[0]))
    for c in sends:
        c.wait_recv()
    for s in range(1, Z):
        mine = Z - s
        j = NEAR.index(mine) if mine in NEAR else FAR.index(mine)
        parts.append((logs_of(lrecv[s], j), orecv[s]))
    peak = parts[0][0]
    for logs, _ in parts[1:]:
        peak = jnp.maximum(peak, logs)
    total, mixed = jnp.zeros((BLOCK, 1), F32), jnp.zeros((BLOCK, HD), F32)
    for logs, value in parts:
        share = jnp.exp(logs - peak)
        total += share
        mixed += share * value
    mine = pl.ds(pl.multiple_of(z * BLOCK, BLOCK), BLOCK)
    att[mine, :] = mixed / total

    spread = [remote(att.at[mine], att.at[mine], c_send.at[d], c_recv.at[d], along(d)) for d in FAR_FIRST]
    for c in spread:
        c.start()
    for c in spread:
        c.wait_recv()

    rows = jnp.concatenate([att[pl.ds(g, 32, stride=8), :] for g in range(8)], axis=1)
    high, low = split2(rows)
    for k in range(QUAD):
        part = nt(high, wh[k]) + nt(low, wh[k]) + nt(high, wl[k])
        for h in range(HEADS):
            psend[k, h] = part[4 * h : 4 * h + 4]
    last = []
    for k, d in mates:
        last.append(
            remote(
                psend.at[k, lax.rem(head + d, HEADS)], precv.at[(HEADS - d) % HEADS, q],
                d_send.at[d * QUAD + k], d_recv.at[d * QUAD + k], in_quad(k, d),
            )
        )
        last[-1].start()
    precv[0, q] = psend[0, head]
    for c in last:
        c.wait_recv()
    summed = precv[0]
    for d in range(1, HEADS):
        summed += precv[d]
    for other in range(QUAD):
        for half in range(2):
            for t in range(2):
                out_ref[t, half * QUAD + other, :] = summed[other, half * 2 + t, :80]
    for c in list(first.values()) + second + y_kv + c_kv + cy_kv + [y_w, c_w, cy_w] + sends + spread + last:
        c.wait_send()


def local(
    queries, prompt_keys, prompt_values, suffix_keys, suffix_values, new_keys, new_values, suffix_lengths, out_weight
):
    dma = pltpu.SemaphoreType.DMA
    return pl.pallas_call(
        kernel,
        out_shape=jax.ShapeDtypeStruct((2, 8, 80), F32),
        in_specs=[pl.BlockSpec(memory_space=pltpu.HBM)] * 9,
        out_specs=pl.BlockSpec(memory_space=pltpu.VMEM),
        scratch_shapes=[
            pltpu.VMEM((Z, BLOCK, HD), F32),
            pltpu.VMEM((QUAD, 2, 256, HD), F32),
            pltpu.VMEM((QUAD, 80, 1024), F32),
            pltpu.VMEM((128, HD), F32),
            pltpu.VMEM((128, HD), F32),
            pltpu.VMEM((2, HD), F32),
            pltpu.VMEM((2, HD), F32),
            pltpu.SMEM((1,), jnp.int32),
            pltpu.VMEM((1024, 256), BF16),
            pltpu.VMEM((1024, 256), BF16),
            pltpu.VMEM((1024, 256), BF16),
            pltpu.VMEM((1024, 256), BF16),
            pltpu.VMEM((QUAD, 128, 1024), BF16),
            pltpu.VMEM((QUAD, 128, 1024), BF16),
            pltpu.VMEM((Z, BLOCK, HD), F32),
            pltpu.VMEM((Z, BLOCK, HD), F32),
            pltpu.VMEM((2, 1, HD), F32),
            pltpu.VMEM((Z, 1, HD), F32),
            pltpu.VMEM((Z * BLOCK, HD), F32),
            pltpu.VMEM((QUAD, HEADS, 4, 128), F32),
            pltpu.VMEM((HEADS, QUAD, 4, 128), F32),
            dma((9,)),
            dma((28,)), dma((28,)),
            dma((9,)), dma((9,)),
            dma((Z,)), dma((Z,)),
            dma((Z,)), dma((Z,)),
            dma((Z,)), dma((Z,)),
            dma((HEADS * QUAD,)), dma((HEADS * QUAD,)),
        ],
        compiler_params=pltpu.CompilerParams(
            collective_id=0, has_side_effects=True, vmem_limit_bytes=60 * 2**20
        ),
    )(
        queries.reshape(BLOCK, HD),
        prompt_keys.reshape(256, HD),
        prompt_values.reshape(256, HD),
        suffix_keys.reshape(128, HD),
        suffix_values.reshape(128, HD),
        new_keys.reshape(2, HD),
        new_values.reshape(2, HD),
        suffix_lengths,
        out_weight.T,
    )


def solution(mesh):
    return jax.shard_map(
        local,
        mesh=mesh,
        in_specs=(
            P(None, "ctx", "head", None),
            P("ctx", "head", None),
            P("ctx", "head", None),
            P("ctx", None, "head", None),
            P("ctx", None, "head", None),
            P(None, "ctx", "head", None),
            P(None, "ctx", "head", None),
            P("ctx"),
            P("head", "ctx"),
        ),
        out_specs=P(None, "head", "ctx"),
        check_vma=False,
    )
```

time: 1050 us -> 56 us (0.05)
  starting transfers between devices: 752 us -> 0 us
  waiting for transfers between devices: 153 us -> 0 us
  blocking collectives: 64.9 us -> 0 us
  Pallas kernels: 0 us -> 53.9 us
  matrix products: 36.6 us -> 0 us
  between operations: 14.1 us -> 0.66 us
  other arithmetic: 13.1 us -> 0 us
    ppermute x256 -> x0, starting transfers between devices: 752 us -> none  [from_behind(): return lax.ppermute(value, axis, pairs)]
    ppermute x256 -> x0, waiting for transfers between devices: 80.1 us -> none  [from_behind(): return lax.ppermute(value, axis, pairs)]
    reduce_scatter x1 -> x0, waiting for transfers between devices: 72.6 us -> none  [local(): lax.psum_scatter(partial_out, 'head', scatter_dimension=1, tiled=True)]
    all_gather x1 -> x0, blocking collectives: 64.9 us -> none  [local(): lax.all_gather(attention, 'ctx', axis=1, tiled=True)]
    pallas_call x0 -> x1, Pallas kernels: none -> 53.9 us  [local(): pl.pallas_call(kernel, out_shape=jax.ShapeDtypeStruct((2, 8, 80), F32), i...]
    dot_general x133 -> x0, matrix products: 36.6 us -> none  [the longest x64 17.8 us: prompt_part(): jnp.einsum('trkgd,pkd->trkgp', query_block, key_rows, precision=HIGHEST)]
    reduce_sum x66 -> x0, other arithmetic: 10.7 us -> none  [the longest x64 10.4 us: prompt_part(): row_total = jnp.sum(weights, axis=-1)]
  transfers between devices with their start and end apart: 257 -> 0, of which waited for: 70 -> 0; matrix products, arithmetic and copies ran while one was open for 4% -> 0% of each run, Pallas kernels for 0% -> 0%
where the time goes in v1:
time: 56 us; the launch traced here: 55.8 us
  Pallas kernels  53.9 us (96%)
  local copies, waits for them, and re-layouts  1.3 us (2%)
  between operations  0.66 us (1%)
    pallas_call x1, Pallas kernels, local(): pl.pallas_call(kernel, out_shape=jax.ShapeDtypeStruct((2, 8, 80), F32), i...  53.9 us
    unnamed x1, local copies, waits for them, and re-layouts  1.3 us

profile of v1, /device:TPU:1, one launch (start us, length us, event | category | flops | bytes accessed | tf_op | source)
XLA Modules:
  0.0 55.8 jit_solution(5051428392134441545)
XLA Ops:
  0.7 53.9 %shard_map.91 = f32[2,8,80]{2,1,0:T(8,128)} custom-call(f32[16,128]{1,0:T(8,128)} %bitcast.13, f32[256,128]{1,0:T(8,128)} %bitcast.9, f32[256,128]{1,0:T(8,128)} %bitcast.10, f32[128,128]{1,0:T(8,128)} %bitcast.11, f32[128,128]{1,0:T(8,128)} %bitcast.12, f32[2,128]{1,0:T(2,128)} %bitcast.14, f32[2,128]{1,0:T(2,128)} %bitcast.15, s32[1]{0:T(128)S(6)} %copy.11.len_in, ...), custom_call_target="tpu_custom_call" | custom-call | tf_op jit(solution)/shard_map/pallas_call | solution.py:263
  54.5 1.3 %copy.12 = f32[2,8,80]{2,1,0:T(8,128)} copy(f32[2,8,80]{2,1,0:T(8,128)} %shard_map.91) | data formatting | bytes 10240

commit v2 on v1

--- a/solution.py
+++ b/solution.py
@@ -11,8 +11,7 @@
 WINDOW = 4
 BLOCK = 16
 HD = 128
-NEAR = (12, 13, 14, 15, 0, 1, 2, 3)
-FAR = (4, 5, 6, 7, 8, 9, 10, 11)
+LOG2E = 1.4426950408889634
 FAR_FIRST = sorted(range(1, Z), key=lambda d: -min(d, Z - d))
 
 
@@ -45,14 +44,18 @@
     ctx, head = lax.axis_index("ctx"), lax.axis_index("head")
     z, q = ctx // QUAD, lax.rem(ctx, QUAD)
     core, side = lax.rem(q, 2), q // 2
+    x, y = lax.rem(head, 4), head // 4
 
     def along(d):
         return (lax.rem(ctx + QUAD * (d % Z), Z * QUAD), head)
+
+    def head_of(d):
+        return (1 - y if d & 4 else y) * 4 + lax.rem(x + (d & 3), 4)
 
     def in_quad(k, d=0):
         c = 1 - core if k & 1 else core
         s = 1 - side if k & 2 else side
-        return (z * QUAD + s * 2 + c, lax.rem(head + d, HEADS))
+        return (z * QUAD + s * 2 + c, head_of(d))
 
     def remote(src, dst, send, recv, to):
         return pltpu.make_async_remote_copy(
@@ -63,9 +66,10 @@
     barrier = pltpu.get_barrier_semaphore()
     for d in window:
         pl.semaphore_signal(barrier, inc=1, device_id=along(d), device_id_type=MESH)
-    mates = [(k, d) for d in (0, 2, 6, 4, 1, 3, 5, 7) for k in (2, 3, 1, 0) if (k, d) != (0, 0)]
-    for k, d in mates:
+    greeted = [(0, 6), (0, 5), (0, 7), (0, 4), (0, 2), (0, 1), (0, 3), (2, 0), (3, 0), (1, 0)]
+    for k, d in greeted:
         pl.semaphore_signal(barrier, inc=1, device_id=in_quad(k, d), device_id_type=MESH)
+    mates = [(k, d) for d in (6, 5, 7, 4, 2, 1, 3, 0) for k in (2, 3, 1, 0) if (k, d) != (0, 0)]
 
     own = [
         pltpu.make_async_copy(src, dst, in_sem.at[i])
@@ -78,22 +82,32 @@
     ]
     for c in own:
         c.start()
-    pl.semaphore_wait(barrier, len(window) + len(mates))
-
-    first = {d: remote(q_in, qbuf.at[Z - d], a_send.at[d], a_recv.at[d], along(d)) for d in window}
+    own[0].wait()
+    own[1].wait()
+    own[2].wait()
+    pl.semaphore_wait(barrier, len(window) + len(greeted))
+
+    first = {d: remote(qbuf.at[0], qbuf.at[Z - d], a_send.at[d], a_recv.at[d], along(d)) for d in window}
     for d in window:
         first[d].start()
-    y_kv = [remote((k_in, v_in)[i], kv.at[2, i], x_send.at[i], x_recv.at[i], in_quad(2)) for i in (0, 1)]
-    c_kv = [remote((k_in, v_in)[i], kv.at[1, i], x_send.at[2 + i], x_recv.at[2 + i], in_quad(1)) for i in (0, 1)]
+    y_kv = [remote(kv.at[0, i], kv.at[2, i], x_send.at[i], x_recv.at[i], in_quad(2)) for i in (0, 1)]
+    c_kv = [remote(kv.at[0, i], kv.at[1, i], x_send.at[2 + i], x_recv.at[2 + i], in_quad(1)) for i in (0, 1)]
     cy_kv = [remote(kv.at[2, i], kv.at[3, i], x_send.at[4 + i], x_recv.at[4 + i], in_quad(1)) for i in (0, 1)]
-    y_w = remote(w_in, w.at[2], x_send.at[6], x_recv.at[6], in_quad(2))
-    c_w = remote(w_in, w.at[1], x_send.at[7], x_recv.at[7], in_quad(1))
+    y_w = remote(w.at[0], w.at[2], x_send.at[6], x_recv.at[6], in_quad(2))
+    c_w = remote(w.at[0], w.at[1], x_send.at[7], x_recv.at[7], in_quad(1))
     cy_w = remote(w.at[2], w.at[3], x_send.at[8], x_recv.at[8], in_quad(1))
     for c in y_kv + c_kv:
         c.start()
-    for c in own:
-        c.wait()
-
+    def prepare(i):
+        rows = pl.ds(i * 256, 256)
+        high, middle, low = split3(kv[i, 0])
+        ka[rows, :] = jnp.concatenate([high, high], axis=1)
+        kb[rows, :] = jnp.concatenate([middle, middle], axis=1)
+        kc[rows, :] = jnp.concatenate([low, high], axis=1)
+        high, low = split2(kv[i, 1])
+        vv[rows, :] = jnp.concatenate([high, low], axis=1)
+
+    prepare(0)
     second = []
     for k in range(1, WINDOW + 1):
         first[Z - k].wait_recv()
@@ -108,81 +122,66 @@
             c.start()
             second.append(c)
 
-    def prepare(i):
-        rows = pl.ds(i * 256, 256)
-        high, middle, low = split3(kv[i, 0])
-        ka[rows, :] = jnp.concatenate([high, high], axis=1)
-        kb[rows, :] = jnp.concatenate([middle, middle], axis=1)
-        kc[rows, :] = jnp.concatenate([low, high], axis=1)
-        high, low = split2(kv[i, 1])
-        vv[rows, :] = jnp.concatenate([high, low], axis=1)
-
-    prepare(0)
+    scale = HD**-0.5 * LOG2E
+    sends = []
+
+    def hand_out(d):
+        sends.append(remote(osend.at[d], orecv.at[Z - d], o_send.at[d], o_recv.at[d], along(d)))
+        sends.append(remote(lsend.at[d // 8], lrecv.at[Z - d], l_send.at[d], l_recv.at[d], along(d)))
+        sends[-2].start()
+        sends[-1].start()
+
     for c in c_kv:
         c.wait_recv()
     prepare(1)
     for i in (0, 1):
         y_kv[i].wait_recv()
         cy_kv[i].start()
+    for c in own[3:]:
+        c.wait()
     y_w.start()
     c_w.start()
     prepare(2)
+    for c in second:
+        c.wait_recv()
+    high, middle, low = split3(qbuf[...].reshape(Z * BLOCK, HD) * scale)
     for c in cy_kv:
         c.wait_recv()
     prepare(3)
-
-    scale = HD**-0.5
-    lane = lax.broadcasted_iota(jnp.int32, (128, 128), 1)
-    row = lax.broadcasted_iota(jnp.int32, (128, 128), 0)
-    sends = []
-
-    def prompt(b, slots):
-        queries = jnp.concatenate([qbuf[s] for s in slots], axis=0)
-        high, middle, low = split3(queries)
-        qa = jnp.concatenate([high, middle], axis=1)
-        qc = jnp.concatenate([high, low], axis=1)
-        scores = nt(qa, ka[...]) + nt(qa, kb[...]) + nt(qc, kc[...])
-        peak = jnp.max(scores, axis=1, keepdims=True)
-        weights = jnp.exp((scores - peak) * scale)
-        total = jnp.sum(weights, axis=1, keepdims=True)
-        high, low = split2(weights)
-        both = nn(high, vv[...]) + nn(low, vv[...])
-        mixed = (both[:, :HD] + both[:, HD:]) / total
-        logs = peak * scale + jnp.log(total)
-        lsend[b] = jnp.sum(jnp.where(lane == row, logs, 0.0), axis=0, keepdims=True)
-        for j, s in enumerate(slots):
-            osend[s] = mixed[j * BLOCK : (j + 1) * BLOCK]
-        for s in sorted(slots, key=lambda s: -min(s, Z - s)):
-            if s:
-                sends.append(remote(osend.at[s], orecv.at[Z - s], o_send.at[s], o_recv.at[s], along(s)))
-                sends.append(remote(lsend.at[b], lrecv.at[Z - s], l_send.at[s], l_recv.at[s], along(s)))
-                sends[-2].start()
-                sends[-1].start()
-
-    prompt(0, NEAR)
-    for c in second:
-        c.wait_recv()
-    prompt(1, FAR)
-
-    queries = qbuf[0]
+    first_two = jnp.concatenate([high, middle], axis=1)
+    scores = nt(first_two, ka[...]) + nt(first_two, kb[...]) + nt(jnp.concatenate([high, low], axis=1), kc[...])
+    peak = jnp.max(scores, axis=1, keepdims=True)
+    weights = jnp.exp2(scores - peak)
+    total = jnp.sum(weights, axis=1, keepdims=True)
+    high, low = split2(weights)
+    both = nn(high, vv[...]) + nn(low, vv[...])
+    osend[...] = ((both[:, :HD] + both[:, HD:]) / total).reshape(Z, BLOCK, HD)
+    lane = lax.broadcasted_iota(jnp.int32, (2, 128, 128), 2)
+    row = lax.broadcasted_iota(jnp.int32, (2, 128, 128), 1)
+    logs = (peak + jnp.log2(total)).reshape(2, 128, 1)
+    lsend[...] = jnp.sum(jnp.where(lane == row, logs, 0.0), axis=1, keepdims=True)
+    for d in FAR_FIRST:
+        hand_out(d)
+
+    queries = qbuf[0] * scale
     high, middle, low = split3(queries)
     kh, km, kl = split3(sk[...])
     scores = nt(high, kh) + nt(middle, kh) + nt(high, km) + nt(middle, km) + nt(high, kl) + nt(low, kh)
     lane16 = lax.broadcasted_iota(jnp.int32, (BLOCK, 128), 1)
     row16 = lax.broadcasted_iota(jnp.int32, (BLOCK, 128), 0)
-    scores = jnp.where(lane16 < length[0], scores * scale, -1e30)
+    scores = jnp.where(lane16 < length[0], scores, -1e30)
     fresh = nk[...]
-    new0 = jnp.sum(queries * fresh[0:1], axis=1, keepdims=True) * scale
-    new1 = jnp.sum(queries * fresh[1:2], axis=1, keepdims=True) * scale
+    new0 = jnp.sum(queries * fresh[0:1], axis=1, keepdims=True)
+    new1 = jnp.sum(queries * fresh[1:2], axis=1, keepdims=True)
     new1 = jnp.where(row16[:, :1] >= 8, new1, -1e30)
     peak = jnp.maximum(jnp.max(scores, axis=1, keepdims=True), jnp.maximum(new0, new1))
-    weights, new0, new1 = jnp.exp(scores - peak), jnp.exp(new0 - peak), jnp.exp(new1 - peak)
+    weights, new0, new1 = jnp.exp2(scores - peak), jnp.exp2(new0 - peak), jnp.exp2(new1 - peak)
     total = jnp.sum(weights, axis=1, keepdims=True) + new0 + new1
     wth, wtl = split2(weights)
     vh, vl = split2(sv[...])
     fresh = nv[...]
     mixed = nn(wth, vh) + nn(wth, vl) + nn(wtl, vh) + new0 * fresh[0:1] + new1 * fresh[1:2]
-    parts = [(peak + jnp.log(total), mixed / total)]
+    parts = [(peak + jnp.log2(total), mixed / total)]
 
     def columns(k):
         high, low = split2(w[k])
@@ -203,19 +202,18 @@
     def logs_of(values, j):
         return jnp.sum(jnp.where(lane16 == row16 + BLOCK * j, values, 0.0), axis=1, keepdims=True)
 
-    parts.append((logs_of(lsend[0], NEAR.index(0)), osend[0]))
+    parts.append((logs_of(lsend[0], 0), osend[0]))
     for c in sends:
         c.wait_recv()
     for s in range(1, Z):
         mine = Z - s
-        j = NEAR.index(mine) if mine in NEAR else FAR.index(mine)
-        parts.append((logs_of(lrecv[s], j), orecv[s]))
+        parts.append((logs_of(lrecv[s], mine % 8), orecv[s]))
     peak = parts[0][0]
     for logs, _ in parts[1:]:
         peak = jnp.maximum(peak, logs)
     total, mixed = jnp.zeros((BLOCK, 1), F32), jnp.zeros((BLOCK, HD), F32)
     for logs, value in parts:
-        share = jnp.exp(logs - peak)
+        share = jnp.exp2(logs - peak)
         total += share
         mixed += share * value
     mine = pl.ds(pl.multiple_of(z * BLOCK, BLOCK), BLOCK)
@@ -229,15 +227,17 @@
 
     rows = jnp.concatenate([att[pl.ds(g, 32, stride=8), :] for g in range(8)], axis=1)
     high, low = split2(rows)
+    halves = jnp.concatenate([high, low], axis=0)
     for k in range(QUAD):
-        part = nt(high, wh[k]) + nt(low, wh[k]) + nt(high, wl[k])
+        part = nt(halves, wh[k])
+        part = part[:32] + part[32:] + nt(high, wl[k])
         for h in range(HEADS):
             psend[k, h] = part[4 * h : 4 * h + 4]
     last = []
     for k, d in mates:
         last.append(
             remote(
-                psend.at[k, lax.rem(head + d, HEADS)], precv.at[(HEADS - d) % HEADS, q],
+                psend.at[k, head_of(d)], precv.at[(d & 4) + (4 - (d & 3)) % 4, q],
                 d_send.at[d * QUAD + k], d_recv.at[d * QUAD + k], in_quad(k, d),
             )
         )
@@ -262,7 +262,7 @@
     dma = pltpu.SemaphoreType.DMA
     return pl.pallas_call(
         kernel,
-        out_shape=jax.ShapeDtypeStruct((2, 8, 80), F32),
+        out_shape=pltpu.VMEM((2, 8, 80), F32),
         in_specs=[pl.BlockSpec(memory_space=pltpu.HBM)] * 9,
         out_specs=pl.BlockSpec(memory_space=pltpu.VMEM),
         scratch_shapes=[

time: 56 us -> 51.6 us (0.921)
  Pallas kernels: 53.9 us -> 50.2 us
  local copies, waits for them, and re-layouts: 1.3 us -> 0.6 us
    pallas_call x1, Pallas kernels: 53.9 us -> 50.2 us  [local(): pl.pallas_call(kernel, out_shape=pltpu.VMEM((2, 8, 80), F32), in_specs=[p...]
    unnamed x1, local copies, waits for them, and re-layouts: 1.3 us -> 0.6 us
where the time goes in v2:
time: 51.6 us; the launch traced here: 51.4 us
  Pallas kernels  50.2 us (97%)
  between operations  0.66 us (1%)
  local copies, waits for them, and re-layouts  0.6 us (1%)
    pallas_call x1, Pallas kernels, local(): pl.pallas_call(kernel, out_shape=pltpu.VMEM((2, 8, 80), F32), in_specs=[p...  50.2 us

profile of v2, /device:TPU:1, one launch (start us, length us, event | category | flops | bytes accessed | tf_op | source)
XLA Modules:
  0.0 51.4 jit_solution(1658974194243537733)
XLA Ops:
  0.7 50.2 %shard_map.91 = f32[2,8,80]{2,1,0:T(8,128)S(1)} custom-call(f32[16,128]{1,0:T(8,128)} %bitcast.13, f32[256,128]{1,0:T(8,128)} %bitcast.9, f32[256,128]{1,0:T(8,128)} %bitcast.10, f32[128,128]{1,0:T(8,128)} %bitcast.11, f32[128,128]{1,0:T(8,128)} %bitcast.12, f32[2,128]{1,0:T(2,128)} %bitcast.14, f32[2,128]{1,0:T(2,128)} %bitcast.15, s32[1]{0:T(128)S(6)} %copy.12.len_in, ...), custom_call_target="tpu_custom_call" | custom-call | tf_op jit(solution)/shard_map/pallas_call | solution.py:263
  50.8 0.6 %copy.11 = f32[2,8,80]{2,1,0:T(8,128)} copy(f32[2,8,80]{2,1,0:T(8,128)S(1)} %shard_map.91) | data formatting | bytes 10240

commit v3 on v2

v3 whole, which is shorter than its diff:
```python
import jax
import jax.numpy as jnp
from jax import lax
from jax.experimental import pallas as pl
from jax.experimental.pallas import tpu as pltpu
from jax.sharding import PartitionSpec as P

MESH = pl.DeviceIdType.MESH
F32, BF16 = jnp.float32, jnp.bfloat16
Z, QUAD, HEADS = 16, 4, 8
WINDOW = 4
BLOCK = 16
HD = 128
LOG2E = 1.4426950408889634
FAR_FIRST = sorted(range(1, Z), key=lambda d: -min(d, Z - d))
(
    IN_Q, IN_KV, IN_SUF, IN_NEW, IN_LEN, IN_W, A_SEND, A_UP, A_DOWN, A_NEAR, A2_SEND, A2_RECV, KV_SEND, YK, YV, CKV,
    CYKV, W_SEND, YW, CW, CYW, B_SEND, B_RECV, C_SEND, C_RECV, D_SEND, D_RECV, SEMS,
) = range(28)


def nt(a, b):
    return lax.dot_general(a, b, (((1,), (1,)), ((), ())), preferred_element_type=F32)


def nn(a, b):
    return jnp.dot(a, b, preferred_element_type=F32)


def split2(x):
    high = x.astype(BF16)
    return high, (x - high.astype(F32)).astype(BF16)


def split3(x):
    high = x.astype(BF16)
    rest = x - high.astype(F32)
    middle = rest.astype(BF16)
    return high, middle, (rest - middle.astype(F32)).astype(BF16)


def kernel(
    q_in, k_in, v_in, sk_in, sv_in, nk_in, nv_in, len_in, w_in, out_ref,
    qbuf, kv, w, suf, new, length, ka, kb, kc, vv, wh, wl, osend, orecv, att, psend, precv, sem,
):
    ctx, head = lax.axis_index("ctx"), lax.axis_index("head")
    z, q = ctx // QUAD, lax.rem(ctx, QUAD)
    core, side = lax.rem(q, 2), q // 2
    x, y = lax.rem(head, 4), head // 4

    def along(d):
        return (lax.rem(ctx + QUAD * (d % Z), Z * QUAD), head)

    def head_of(d):
        return (1 - y if d & 4 else y) * 4 + lax.rem(x + (d & 3), 4)

    def in_quad(k, d=0):
        c = 1 - core if k & 1 else core
        s = 1 - side if k & 2 else side
        return (z * QUAD + s * 2 + c, head_of(d))

    def remote(src, dst, send, recv, to):
        return pltpu.make_async_remote_copy(
            src_ref=src, dst_ref=dst, send_sem=sem.at[send], recv_sem=sem.at[recv], device_id=to, device_id_type=MESH
        )

    def put(src, dst, send, recv, to):
        remote(src, dst, send, recv, to).start()

    def arrived(ref, recv):
        remote(ref, ref, recv, recv, in_quad(1)).wait_recv()

    def sent(ref, send):
        remote(ref, ref, send, send, in_quad(1)).wait_send()

    window = [d for d in FAR_FIRST if min(d, Z - d) <= WINDOW]
    barrier = pltpu.get_barrier_semaphore()
    for d in window:
        pl.semaphore_signal(barrier, inc=1, device_id=along(d), device_id_type=MESH)
    greeted = [(0, 6), (0, 5), (0, 7), (0, 4), (0, 2), (0, 1), (0, 3), (2, 0), (3, 0), (1, 0)]
    for k, d in greeted:
        pl.semaphore_signal(barrier, inc=1, device_id=in_quad(k, d), device_id_type=MESH)

    own = [
        pltpu.make_async_copy(src, dst, sem.at[i])
        for src, dst, i in (
            (q_in, qbuf.at[0], IN_Q), (k_in, kv.at[0, 0], IN_KV), (v_in, kv.at[0, 1], IN_KV),
            (sk_in, suf.at[0], IN_SUF), (sv_in, suf.at[1], IN_SUF), (nk_in, new.at[0], IN_NEW),
            (nv_in, new.at[1], IN_NEW), (len_in, length, IN_LEN), (w_in, w.at[0], IN_W),
        )
    ]
    for c in own:
        c.start()

    def loaded(ref, i):
        pltpu.make_async_copy(ref, ref, sem.at[i]).wait()

    loaded(qbuf.at[0], IN_Q)
    loaded(kv.at[0], IN_KV)
    pl.semaphore_wait(barrier, len(window) + len(greeted))

    for d in window:
        recv = A_UP if d == Z - WINDOW else A_DOWN if d == WINDOW else A_NEAR
        put(qbuf.at[0], qbuf.at[Z - d], A_SEND, recv, along(d))
    put(kv.at[0, 0], kv.at[2, 0], KV_SEND, YK, in_quad(2))
    put(kv.at[0, 1], kv.at[2, 1], KV_SEND, YV, in_quad(2))
    put(kv.at[0, 0], kv.at[1, 0], KV_SEND, CKV, in_quad(1))
    put(kv.at[0, 1], kv.at[1, 1], KV_SEND, CKV, in_quad(1))

    def prepare(i):
        rows = pl.ds(i * 256, 256)
        high, middle, low = split3(kv[i, 0])
        ka[rows, :] = jnp.concatenate([high, high], axis=1)
        kb[rows, :] = jnp.concatenate([middle, middle], axis=1)
        kc[rows, :] = jnp.concatenate([low, high], axis=1)
        high, low = split2(kv[i, 1])
        vv[rows, :] = jnp.concatenate([high, low], axis=1)

    prepare(0)
    for held, recv, hops in ((WINDOW, A_UP, (-4, -3, -2, -1)), (Z - WINDOW, A_DOWN, (3, 2, 1))):
        arrived(qbuf.at[held], recv)
        for d in hops:
            put(qbuf.at[held], qbuf.at[(held - d) % Z], A2_SEND, A2_RECV, along(d))
    arrived(qbuf.at[pl.ds(1, 6)], A_NEAR)

    arrived(kv.at[1], CKV)
    prepare(1)
    for i, recv in ((0, YK), (1, YV)):
        arrived(kv.at[2, i], recv)
        put(kv.at[2, i], kv.at[3, i], KV_SEND, CYKV, in_quad(1))
    loaded(w.at[0], IN_W)
    put(w.at[0], w.at[2], W_SEND, YW, in_quad(2))
    put(w.at[0], w.at[1], W_SEND, CW, in_quad(1))
    prepare(2)
    arrived(qbuf.at[pl.ds(5, 7)], A2_RECV)
    scale = HD**-0.5 * LOG2E
    high, middle, low = split3(qbuf[...].reshape(Z * BLOCK, HD) * scale)
    arrived(kv.at[3], CYKV)
    prepare(3)
    first_two = jnp.concatenate([high, middle], axis=1)
    scores = nt(first_two, ka[...]) + nt(first_two, kb[...]) + nt(jnp.concatenate([high, low], axis=1), kc[...])
    peak = jnp.max(scores, axis=1, keepdims=True)
    weights = jnp.exp2(scores - peak)
    total = jnp.sum(weights, axis=1, keepdims=True)
    high, low = split2(weights)
    both = nn(high, vv[...]) + nn(low, vv[...])
    osend[:, :BLOCK] = ((both[:, :HD] + both[:, HD:]) / total).reshape(Z, BLOCK, HD)
    lane = lax.broadcasted_iota(jnp.int32, (2, 128, 128), 2)
    row = lax.broadcasted_iota(jnp.int32, (2, 128, 128), 1)
    logs = (peak + jnp.log2(total)).reshape(2, 128, 1)
    logs = jnp.sum(jnp.where(lane == row, logs, 0.0), axis=1, keepdims=True)
    for d in range(Z):
        osend[d, BLOCK:] = logs[d // 8]
    for d in FAR_FIRST:
        put(osend.at[d], orecv.at[Z - d], B_SEND, B_RECV, along(d))

    loaded(suf, IN_SUF)
    loaded(new, IN_NEW)
    loaded(length, IN_LEN)
    queries = qbuf[0] * scale
    high, middle, low = split3(queries)
    kh, km, kl = split3(suf[0])
    scores = nt(high, kh) + nt(middle, kh) + nt(high, km) + nt(middle, km) + nt(high, kl) + nt(low, kh)
    lane16 = lax.broadcasted_iota(jnp.int32, (BLOCK, 128), 1)
    row16 = lax.broadcasted_iota(jnp.int32, (BLOCK, 128), 0)
    scores = jnp.where(lane16 < length[0], scores, -1e30)
    fresh = new[0]
    new0 = jnp.sum(queries * fresh[0:1], axis=1, keepdims=True)
    new1 = jnp.sum(queries * fresh[1:2], axis=1, keepdims=True)
    new1 = jnp.where(row16[:, :1] >= 8, new1, -1e30)
    peak = jnp.maximum(jnp.max(scores, axis=1, keepdims=True), jnp.maximum(new0, new1))
    weights, new0, new1 = jnp.exp2(scores - peak), jnp.exp2(new0 - peak), jnp.exp2(new1 - peak)
    total = jnp.sum(weights, axis=1, keepdims=True) + new0 + new1
    wth, wtl = split2(weights)
    vh, vl = split2(suf[1])
    fresh = new[1]
    mixed = nn(wth, vh) + nn(wth, vl) + nn(wtl, vh) + new0 * fresh[0:1] + new1 * fresh[1:2]
    parts = [(peak + jnp.log2(total), mixed / total)]

    def columns(k):
        high, low = split2(w[k])
        wh[k, 0:80] = high
        wl[k, 0:80] = low
        wh[k, 80:128] = jnp.zeros((48, 1024), BF16)
        wl[k, 80:128] = jnp.zeros((48, 1024), BF16)

    columns(0)
    arrived(w.at[1], CW)
    columns(1)
    arrived(w.at[2], YW)
    put(w.at[2], w.at[3], W_SEND, CYW, in_quad(1))
    columns(2)
    arrived(w.at[3], CYW)
    columns(3)
    sent(qbuf.at[pl.ds(0, 8)], A_SEND)
    sent(qbuf.at[pl.ds(0, 7)], A2_SEND)
    sent(kv.at[pl.ds(0, 3)], KV_SEND)
    sent(w.at[pl.ds(0, 3)], W_SEND)

    def logs_of(values, j):
        return jnp.sum(jnp.where(lane16 == row16 + BLOCK * j, values, 0.0), axis=1, keepdims=True)

    parts.append((logs_of(osend[0, BLOCK:], 0), osend[0, :BLOCK]))
    arrived(orecv.at[pl.ds(1, Z - 1)], B_RECV)
    for s in range(1, Z):
        mine = Z - s
        parts.append((logs_of(orecv[s, BLOCK:], mine % 8), orecv[s, :BLOCK]))
    peak = parts[0][0]
    for logs, _ in parts[1:]:
        peak = jnp.maximum(peak, logs)
    total, mixed = jnp.zeros((BLOCK, 1), F32), jnp.zeros((BLOCK, HD), F32)
    for logs, value in parts:
        share = jnp.exp2(logs - peak)
        total += share
        mixed += share * value
    mine = pl.ds(pl.multiple_of(z * BLOCK, BLOCK), BLOCK)
    att[mine, :] = mixed / total

    for d in FAR_FIRST:
        put(att.at[mine], att.at[mine], C_SEND, C_RECV, along(d))
    sent(osend.at[pl.ds(1, Z - 1)], B_SEND)
    arrived(att.at[pl.ds(0, (Z - 1) * BLOCK)], C_RECV)

    rows = jnp.concatenate([att[pl.ds(g, 32, stride=8), :] for g in range(8)], axis=1)
    high, low = split2(rows)
    halves = jnp.concatenate([high, low], axis=0)
    for k in (2, 3, 1, 0):
        part = nt(halves, wh[k])
        part = part[:32] + part[32:] + nt(high, wl[k])
        for h in range(HEADS):
            psend[k * HEADS + h] = part[4 * h : 4 * h + 4]
        for d in (6, 5, 7, 4, 2, 1, 3, 0):
            if (k, d) != (0, 0):
                slot = ((d & 4) + (4 - (d & 3)) % 4) * QUAD + q
                put(psend.at[k * HEADS + head_of(d)], precv.at[slot], D_SEND, D_RECV, in_quad(k, d))
    precv[q] = psend[head]
    sent(att.at[pl.ds(0, (Z - 1) * BLOCK)], C_SEND)
    sent(psend.at[pl.ds(0, HEADS * QUAD - 1)], D_SEND)
    arrived(precv.at[pl.ds(0, HEADS * QUAD - 1)], D_RECV)
    for other in range(QUAD):
        summed = precv[other]
        for d in range(1, HEADS):
            summed += precv[d * QUAD + other]
        for half in range(2):
            for t in range(2):
                out_ref[t, half * QUAD + other, :] = summed[half * 2 + t, :80]


def local(
    queries, prompt_keys, prompt_values, suffix_keys, suffix_values, new_keys, new_values, suffix_lengths, out_weight
):
    return pl.pallas_call(
        kernel,
        out_shape=pltpu.VMEM((2, 8, 80), F32),
        in_specs=[pl.BlockSpec(memory_space=pltpu.HBM)] * 9,
        out_specs=pl.BlockSpec(memory_space=pltpu.VMEM),
        scratch_shapes=[
            pltpu.VMEM((Z, BLOCK, HD), F32),
            pltpu.VMEM((QUAD, 2, 256, HD), F32),
            pltpu.VMEM((QUAD, 80, 1024), F32),
            pltpu.VMEM((2, 128, HD), F32),
            pltpu.VMEM((2, 2, HD), F32),
            pltpu.SMEM((1,), jnp.int32),
            pltpu.VMEM((1024, 256), BF16),
            pltpu.VMEM((1024, 256), BF16),
            pltpu.VMEM((1024, 256), BF16),
            pltpu.VMEM((1024, 256), BF16),
            pltpu.VMEM((QUAD, 128, 1024), BF16),
            pltpu.VMEM((QUAD, 128, 1024), BF16),
            pltpu.VMEM((Z, BLOCK + 1, HD), F32),
            pltpu.VMEM((Z, BLOCK + 1, HD), F32),
            pltpu.VMEM((Z * BLOCK, HD), F32),
            pltpu.VMEM((QUAD * HEADS, 4, 128), F32),
            pltpu.VMEM((HEADS * QUAD, 4, 128), F32),
            pltpu.SemaphoreType.DMA((SEMS,)),
        ],
        compiler_params=pltpu.CompilerParams(
            collective_id=0, has_side_effects=True, vmem_limit_bytes=60 * 2**20
        ),
    )(
        queries.reshape(BLOCK, HD),
        prompt_keys.reshape(256, HD),
        prompt_values.reshape(256, HD),
        suffix_keys.reshape(128, HD),
        suffix_values.reshape(128, HD),
        new_keys.reshape(2, HD),
        new_values.reshape(2, HD),
        suffix_lengths,
        out_weight.T,
    )


def solution(mesh):
    return jax.shard_map(
        local,
        mesh=mesh,
        in_specs=(
            P(None, "ctx", "head", None),
            P("ctx", "head", None),
            P("ctx", "head", None),
            P("ctx", None, "head", None),
            P("ctx", None, "head", None),
            P(None, "ctx", "head", None),
            P(None, "ctx", "head", None),
            P("ctx"),
            P("head", "ctx"),
        ),
        out_specs=P(None, "head", "ctx"),
        check_vma=False,
    )
```

time: 51.6 us -> 49.3 us (0.955)
  Pallas kernels: 50.2 us -> 47.9 us
    pallas_call x1, Pallas kernels: 50.2 us -> 47.9 us  [local(): pl.pallas_call(kernel, out_shape=pltpu.VMEM((2, 8, 80), F32), in_specs=[p...]
where the time goes in v3:
time: 49.3 us; the launch traced here: 49.2 us
  Pallas kernels  47.9 us (97%)
  between operations  0.66 us (1%)
  local copies, waits for them, and re-layouts  0.6 us (1%)
    pallas_call x1, Pallas kernels, local(): pl.pallas_call(kernel, out_shape=pltpu.VMEM((2, 8, 80), F32), in_specs=[p...  47.9 us

profile of v3, /device:TPU:1, one launch (start us, length us, event | category | flops | bytes accessed | tf_op | source)
XLA Modules:
  0.0 49.2 jit_solution(17502956674560151181)
XLA Ops:
  0.7 47.9 %shard_map.91 = f32[2,8,80]{2,1,0:T(8,128)S(1)} custom-call(f32[16,128]{1,0:T(8,128)} %bitcast.13, f32[256,128]{1,0:T(8,128)} %bitcast.9, f32[256,128]{1,0:T(8,128)} %bitcast.10, f32[128,128]{1,0:T(8,128)} %bitcast.11, f32[128,128]{1,0:T(8,128)} %bitcast.12, f32[2,128]{1,0:T(2,128)} %bitcast.14, f32[2,128]{1,0:T(2,128)} %bitcast.15, s32[1]{0:T(128)S(6)} %copy.12.len_in, ...), custom_call_target="tpu_custom_call" | custom-call | tf_op jit(solution)/shard_map/pallas_call | solution.py:252
  48.6 0.6 %copy.11 = f32[2,8,80]{2,1,0:T(8,128)} copy(f32[2,8,80]{2,1,0:T(8,128)S(1)} %shard_map.91) | data formatting | bytes 10240

commit v4 on v3

--- a/solution.py
+++ b/solution.py
@@ -135,16 +135,28 @@
     arrived(qbuf.at[pl.ds(5, 7)], A2_RECV)
     scale = HD**-0.5 * LOG2E
     high, middle, low = split3(qbuf[...].reshape(Z * BLOCK, HD) * scale)
+    first_two = jnp.concatenate([high, middle], axis=1)
+    first_last = jnp.concatenate([high, low], axis=1)
+
+    def visit(start, size):
+        rows = pl.ds(start, size)
+        scores = nt(first_two, ka[rows, :]) + nt(first_two, kb[rows, :]) + nt(first_last, kc[rows, :])
+        peak = jnp.max(scores, axis=1, keepdims=True)
+        weights = jnp.exp2(scores - peak)
+        total = jnp.sum(weights, axis=1, keepdims=True)
+        high, low = split2(weights)
+        both = nn(high, vv[rows, :]) + nn(low, vv[rows, :])
+        return peak, total, both[:, :HD] + both[:, HD:]
+
+    peak_a, total_a, mixed_a = visit(0, 768)
     arrived(kv.at[3], CYKV)
     prepare(3)
-    first_two = jnp.concatenate([high, middle], axis=1)
-    scores = nt(first_two, ka[...]) + nt(first_two, kb[...]) + nt(jnp.concatenate([high, low], axis=1), kc[...])
-    peak = jnp.max(scores, axis=1, keepdims=True)
-    weights = jnp.exp2(scores - peak)
-    total = jnp.sum(weights, axis=1, keepdims=True)
-    high, low = split2(weights)
-    both = nn(high, vv[...]) + nn(low, vv[...])
-    osend[:, :BLOCK] = ((both[:, :HD] + both[:, HD:]) / total).reshape(Z, BLOCK, HD)
+    peak_b, total_b, mixed_b = visit(768, 256)
+    peak = jnp.maximum(peak_a, peak_b)
+    share_a, share_b = jnp.exp2(peak_a - peak), jnp.exp2(peak_b - peak)
+    total = total_a * share_a + total_b * share_b
+    mixed = (mixed_a * share_a + mixed_b * share_b) / total
+    osend[:, :BLOCK] = mixed.reshape(Z, BLOCK, HD)
     lane = lax.broadcasted_iota(jnp.int32, (2, 128, 128), 2)
     row = lax.broadcasted_iota(jnp.int32, (2, 128, 128), 1)
     logs = (peak + jnp.log2(total)).reshape(2, 128, 1)
@@ -189,13 +201,9 @@
     columns(1)
     arrived(w.at[2], YW)
     put(w.at[2], w.at[3], W_SEND, CYW, in_quad(1))
-    columns(2)
-    arrived(w.at[3], CYW)
-    columns(3)
     sent(qbuf.at[pl.ds(0, 8)], A_SEND)
     sent(qbuf.at[pl.ds(0, 7)], A2_SEND)
     sent(kv.at[pl.ds(0, 3)], KV_SEND)
-    sent(w.at[pl.ds(0, 3)], W_SEND)
 
     def logs_of(values, j):
         return jnp.sum(jnp.where(lane16 == row16 + BLOCK * j, values, 0.0), axis=1, keepdims=True)
@@ -219,6 +227,10 @@
     for d in FAR_FIRST:
         put(att.at[mine], att.at[mine], C_SEND, C_RECV, along(d))
     sent(osend.at[pl.ds(1, Z - 1)], B_SEND)
+    columns(2)
+    arrived(w.at[3], CYW)
+    columns(3)
+    sent(w.at[pl.ds(0, 3)], W_SEND)
     arrived(att.at[pl.ds(0, (Z - 1) * BLOCK)], C_RECV)
 
     rows = jnp.concatenate([att[pl.ds(g, 32, stride=8), :] for g in range(8)], axis=1)

time: 49.3 us -> 48.1 us (0.976)
  Pallas kernels: 47.9 us -> 46.7 us
    pallas_call x1, Pallas kernels: 47.9 us -> 46.7 us  [local(): pl.pallas_call(kernel, out_shape=pltpu.VMEM((2, 8, 80), F32), in_specs=[p...]
where the time goes in v4:
time: 48.1 us; the launch traced here: 48 us
  Pallas kernels  46.7 us (97%)
  between operations  0.66 us (1%)
  local copies, waits for them, and re-layouts  0.6 us (1%)
    pallas_call x1, Pallas kernels, local(): pl.pallas_call(kernel, out_shape=pltpu.VMEM((2, 8, 80), F32), in_specs=[p...  46.7 us

profile of v4, /device:TPU:1, one launch (start us, length us, event | category | flops | bytes accessed | tf_op | source)
XLA Modules:
  0.0 48.0 jit_solution(9930153435301647234)
XLA Ops:
  0.7 46.7 %shard_map.91 = f32[2,8,80]{2,1,0:T(8,128)S(1)} custom-call(f32[16,128]{1,0:T(8,128)} %bitcast.13, f32[256,128]{1,0:T(8,128)} %bitcast.9, f32[256,128]{1,0:T(8,128)} %bitcast.10, f32[128,128]{1,0:T(8,128)} %bitcast.11, f32[128,128]{1,0:T(8,128)} %bitcast.12, f32[2,128]{1,0:T(2,128)} %bitcast.14, f32[2,128]{1,0:T(2,128)} %bitcast.15, s32[1]{0:T(128)S(6)} %copy.12.len_in, ...), custom_call_target="tpu_custom_call" | custom-call | tf_op jit(solution)/shard_map/pallas_call | solution.py:264
  47.3 0.6 %copy.11 = f32[2,8,80]{2,1,0:T(8,128)} copy(f32[2,8,80]{2,1,0:T(8,128)S(1)} %shard_map.91) | data formatting | bytes 10240

commit v5 on v4

--- a/solution.py
+++ b/solution.py
@@ -15,8 +15,8 @@
 FAR_FIRST = sorted(range(1, Z), key=lambda d: -min(d, Z - d))
 (
     IN_Q, IN_KV, IN_SUF, IN_NEW, IN_LEN, IN_W, A_SEND, A_UP, A_DOWN, A_NEAR, A2_SEND, A2_RECV, KV_SEND, YK, YV, CKV,
-    CYKV, W_SEND, YW, CW, CYW, B_SEND, B_RECV, C_SEND, C_RECV, D_SEND, D_RECV, SEMS,
-) = range(28)
+    CYK, CYV, W_SEND, YW, CW, CYW, B_SEND, B_RECV, C_SEND, C_RECV, D_SEND, D_RECV, SEMS,
+) = range(29)
 
 
 def nt(a, b):
@@ -99,22 +99,28 @@
     loaded(kv.at[0], IN_KV)
     pl.semaphore_wait(barrier, len(window) + len(greeted))
 
+    put(kv.at[0, 0], kv.at[2, 0], KV_SEND, YK, in_quad(2))
+    put(kv.at[0, 0], kv.at[1, 0], KV_SEND, CKV, in_quad(1))
+    put(kv.at[0, 1], kv.at[2, 1], KV_SEND, YV, in_quad(2))
+    put(kv.at[0, 1], kv.at[1, 1], KV_SEND, CKV, in_quad(1))
+
     for d in window:
         recv = A_UP if d == Z - WINDOW else A_DOWN if d == WINDOW else A_NEAR
         put(qbuf.at[0], qbuf.at[Z - d], A_SEND, recv, along(d))
-    put(kv.at[0, 0], kv.at[2, 0], KV_SEND, YK, in_quad(2))
-    put(kv.at[0, 1], kv.at[2, 1], KV_SEND, YV, in_quad(2))
-    put(kv.at[0, 0], kv.at[1, 0], KV_SEND, CKV, in_quad(1))
-    put(kv.at[0, 1], kv.at[1, 1], KV_SEND, CKV, in_quad(1))
-
-    def prepare(i):
+    def prepare_keys(i):
         rows = pl.ds(i * 256, 256)
         high, middle, low = split3(kv[i, 0])
         ka[rows, :] = jnp.concatenate([high, high], axis=1)
         kb[rows, :] = jnp.concatenate([middle, middle], axis=1)
         kc[rows, :] = jnp.concatenate([low, high], axis=1)
+
+    def prepare_values(i):
         high, low = split2(kv[i, 1])
-        vv[rows, :] = jnp.concatenate([high, low], axis=1)
+        vv[pl.ds(i * 256, 256), :] = jnp.concatenate([high, low], axis=1)
+
+    def prepare(i):
+        prepare_keys(i)
+        prepare_values(i)
 
     prepare(0)
     for held, recv, hops in ((WINDOW, A_UP, (-4, -3, -2, -1)), (Z - WINDOW, A_DOWN, (3, 2, 1))):
@@ -127,7 +133,7 @@
     prepare(1)
     for i, recv in ((0, YK), (1, YV)):
         arrived(kv.at[2, i], recv)
-        put(kv.at[2, i], kv.at[3, i], KV_SEND, CYKV, in_quad(1))
+        put(kv.at[2, i], kv.at[3, i], KV_SEND, CYK + i, in_quad(1))
     loaded(w.at[0], IN_W)
     put(w.at[0], w.at[2], W_SEND, YW, in_quad(2))
     put(w.at[0], w.at[1], W_SEND, CW, in_quad(1))
@@ -138,34 +144,41 @@
     first_two = jnp.concatenate([high, middle], axis=1)
     first_last = jnp.concatenate([high, low], axis=1)
 
-    def visit(start, size):
-        rows = pl.ds(start, size)
+    def weigh(rows):
         scores = nt(first_two, ka[rows, :]) + nt(first_two, kb[rows, :]) + nt(first_last, kc[rows, :])
         peak = jnp.max(scores, axis=1, keepdims=True)
         weights = jnp.exp2(scores - peak)
-        total = jnp.sum(weights, axis=1, keepdims=True)
-        high, low = split2(weights)
-        both = nn(high, vv[rows, :]) + nn(low, vv[rows, :])
-        return peak, total, both[:, :HD] + both[:, HD:]
-
-    peak_a, total_a, mixed_a = visit(0, 768)
-    arrived(kv.at[3], CYKV)
-    prepare(3)
-    peak_b, total_b, mixed_b = visit(768, 256)
+        return peak, jnp.sum(weights, axis=1, keepdims=True), split2(weights)
+
+    def mix(weights, rows):
+        both = nn(weights[0], vv[rows, :]) + nn(weights[1], vv[rows, :])
+        return both[:, :HD] + both[:, HD:]
+
+    early, late = pl.ds(0, 768), pl.ds(768, 256)
+    peak_a, total_a, weights = weigh(early)
+    mixed_a = mix(weights, early)
+    arrived(kv.at[3, 0], CYK)
+    prepare_keys(3)
+    peak_b, total_b, weights = weigh(late)
     peak = jnp.maximum(peak_a, peak_b)
     share_a, share_b = jnp.exp2(peak_a - peak), jnp.exp2(peak_b - peak)
     total = total_a * share_a + total_b * share_b
-    mixed = (mixed_a * share_a + mixed_b * share_b) / total
-    osend[:, :BLOCK] = mixed.reshape(Z, BLOCK, HD)
+    mixed_a *= share_a / total
+    share_b /= total
     lane = lax.broadcasted_iota(jnp.int32, (2, 128, 128), 2)
     row = lax.broadcasted_iota(jnp.int32, (2, 128, 128), 1)
     logs = (peak + jnp.log2(total)).reshape(2, 128, 1)
     logs = jnp.sum(jnp.where(lane == row, logs, 0.0), axis=1, keepdims=True)
     for d in range(Z):
         osend[d, BLOCK:] = logs[d // 8]
+    arrived(kv.at[3, 1], CYV)
+    prepare_values(3)
+    mixed = mixed_a + mix(weights, late) * share_b
+    osend[:, :BLOCK] = mixed.reshape(Z, BLOCK, HD)
     for d in FAR_FIRST:
         put(osend.at[d], orecv.at[Z - d], B_SEND, B_RECV, along(d))
 
+    psend[...] = jnp.zeros_like(psend)
     loaded(suf, IN_SUF)
     loaded(new, IN_NEW)
     loaded(length, IN_LEN)
@@ -190,11 +203,7 @@
     parts = [(peak + jnp.log2(total), mixed / total)]
 
     def columns(k):
-        high, low = split2(w[k])
-        wh[k, 0:80] = high
-        wl[k, 0:80] = low
-        wh[k, 80:128] = jnp.zeros((48, 1024), BF16)
-        wl[k, 80:128] = jnp.zeros((48, 1024), BF16)
+        wh[k], wl[k] = split2(w[k])
 
     columns(0)
     arrived(w.at[1], CW)
@@ -240,7 +249,7 @@
         part = nt(halves, wh[k])
         part = part[:32] + part[32:] + nt(high, wl[k])
         for h in range(HEADS):
-            psend[k * HEADS + h] = part[4 * h : 4 * h + 4]
+            psend[k * HEADS + h, :, :80] = part[4 * h : 4 * h + 4]
         for d in (6, 5, 7, 4, 2, 1, 3, 0):
             if (k, d) != (0, 0):
                 slot = ((d & 4) + (4 - (d & 3)) % 4) * QUAD + q
@@ -277,8 +286,8 @@
             pltpu.VMEM((1024, 256), BF16),
             pltpu.VMEM((1024, 256), BF16),
             pltpu.VMEM((1024, 256), BF16),
-            pltpu.VMEM((QUAD, 128, 1024), BF16),
-            pltpu.VMEM((QUAD, 128, 1024), BF16),
+            pltpu.VMEM((QUAD, 80, 1024), BF16),
+            pltpu.VMEM((QUAD, 80, 1024), BF16),
             pltpu.VMEM((Z, BLOCK + 1, HD), F32),
             pltpu.VMEM((Z, BLOCK + 1, HD), F32),
             pltpu.VMEM((Z * BLOCK, HD), F32),

time: 48.1 us -> 47.8 us (level)
  no operation moved by 1% of the time
where the time goes in v5:
time: 47.8 us; the launch traced here: 47.6 us
  Pallas kernels  46.4 us (97%)
  between operations  0.66 us (1%)
  local copies, waits for them, and re-layouts  0.6 us (1%)
    pallas_call x1, Pallas kernels, local(): pl.pallas_call(kernel, out_shape=pltpu.VMEM((2, 8, 80), F32), in_specs=[p...  46.4 us

profile of v5, /device:TPU:1, one launch (start us, length us, event | category | flops | bytes accessed | tf_op | source)
XLA Modules:
  0.0 47.6 jit_solution(15835305882317161972)
XLA Ops:
  0.7 46.4 %shard_map.91 = f32[2,8,80]{2,1,0:T(8,128)S(1)} custom-call(f32[16,128]{1,0:T(8,128)} %bitcast.13, f32[256,128]{1,0:T(8,128)} %bitcast.9, f32[256,128]{1,0:T(8,128)} %bitcast.10, f32[128,128]{1,0:T(8,128)} %bitcast.11, f32[128,128]{1,0:T(8,128)} %bitcast.12, f32[2,128]{1,0:T(2,128)} %bitcast.14, f32[2,128]{1,0:T(2,128)} %bitcast.15, s32[1]{0:T(128)S(6)} %copy.12.len_in, ...), custom_call_target="tpu_custom_call" | custom-call | tf_op jit(solution)/shard_map/pallas_call | solution.py:273
  47.0 0.6 %copy.11 = f32[2,8,80]{2,1,0:T(8,128)} copy(f32[2,8,80]{2,1,0:T(8,128)S(1)} %shard_map.91) | data formatting | bytes 10240

commit v6 on v5

--- a/solution.py
+++ b/solution.py
@@ -14,9 +14,9 @@
 LOG2E = 1.4426950408889634
 FAR_FIRST = sorted(range(1, Z), key=lambda d: -min(d, Z - d))
 (
-    IN_Q, IN_KV, IN_SUF, IN_NEW, IN_LEN, IN_W, A_SEND, A_UP, A_DOWN, A_NEAR, A2_SEND, A2_RECV, KV_SEND, YK, YV, CKV,
+    IN_Q, IN_KV, IN_SUF, IN_NEW, IN_LEN, IN_W, A_SEND, A_UP, A_DOWN, A_NEAR, A2_RECV, KV_SEND, YK, YV, CKV,
     CYK, CYV, W_SEND, YW, CW, CYW, B_SEND, B_RECV, C_SEND, C_RECV, D_SEND, D_RECV, SEMS,
-) = range(29)
+) = range(28)
 
 
 def nt(a, b):
@@ -89,7 +89,7 @@
             (nv_in, new.at[1], IN_NEW), (len_in, length, IN_LEN), (w_in, w.at[0], IN_W),
         )
     ]
-    for c in own:
+    for c in own[:3]:
         c.start()
 
     def loaded(ref, i):
@@ -122,11 +122,13 @@
         prepare_keys(i)
         prepare_values(i)
 
+    for c in own[3:]:
+        c.start()
     prepare(0)
     for held, recv, hops in ((WINDOW, A_UP, (-4, -3, -2, -1)), (Z - WINDOW, A_DOWN, (3, 2, 1))):
         arrived(qbuf.at[held], recv)
         for d in hops:
-            put(qbuf.at[held], qbuf.at[(held - d) % Z], A2_SEND, A2_RECV, along(d))
+            put(qbuf.at[held], qbuf.at[(held - d) % Z], A_SEND, A2_RECV, along(d))
     arrived(qbuf.at[pl.ds(1, 6)], A_NEAR)
 
     arrived(kv.at[1], CKV)
@@ -210,8 +212,7 @@
     columns(1)
     arrived(w.at[2], YW)
     put(w.at[2], w.at[3], W_SEND, CYW, in_quad(1))
-    sent(qbuf.at[pl.ds(0, 8)], A_SEND)
-    sent(qbuf.at[pl.ds(0, 7)], A2_SEND)
+    sent(qbuf.at[pl.ds(0, 15)], A_SEND)
     sent(kv.at[pl.ds(0, 3)], KV_SEND)
 
     def logs_of(values, j):

time: 47.8 us -> 47.8 us (level)
  no operation moved by 1% of the time
where the time goes in v6:
time: 47.8 us; the launch traced here: 47.6 us
  Pallas kernels  46.4 us (97%)
  between operations  0.66 us (1%)
  local copies, waits for them, and re-layouts  0.6 us (1%)
    pallas_call x1, Pallas kernels, local(): pl.pallas_call(kernel, out_shape=pltpu.VMEM((2, 8, 80), F32), in_specs=[p...  46.4 us

profile of v6, /device:TPU:1, one launch (start us, length us, event | category | flops | bytes accessed | tf_op | source)
XLA Modules:
  0.0 47.6 jit_solution(6823232478073661365)
XLA Ops:
  0.7 46.4 %shard_map.91 = f32[2,8,80]{2,1,0:T(8,128)S(1)} custom-call(f32[16,128]{1,0:T(8,128)} %bitcast.13, f32[256,128]{1,0:T(8,128)} %bitcast.9, f32[256,128]{1,0:T(8,128)} %bitcast.10, f32[128,128]{1,0:T(8,128)} %bitcast.11, f32[128,128]{1,0:T(8,128)} %bitcast.12, f32[2,128]{1,0:T(2,128)} %bitcast.14, f32[2,128]{1,0:T(2,128)} %bitcast.15, s32[1]{0:T(128)S(6)} %copy.12.len_in, ...), custom_call_target="tpu_custom_call" | custom-call | tf_op jit(solution)/shard_map/pallas_call | solution.py:274
  47.0 0.6 %copy.11 = f32[2,8,80]{2,1,0:T(8,128)} copy(f32[2,8,80]{2,1,0:T(8,128)S(1)} %shard_map.91) | data formatting | bytes 10240

commit v7 on v5

--- a/solution.py
+++ b/solution.py
@@ -173,10 +173,18 @@
         osend[d, BLOCK:] = logs[d // 8]
     arrived(kv.at[3, 1], CYV)
     prepare_values(3)
-    mixed = mixed_a + mix(weights, late) * share_b
-    osend[:, :BLOCK] = mixed.reshape(Z, BLOCK, HD)
-    for d in FAR_FIRST:
-        put(osend.at[d], orecv.at[Z - d], B_SEND, B_RECV, along(d))
+
+    def hand_out(first, last):
+        rows = slice(first * BLOCK, last * BLOCK)
+        mixed = mixed_a[rows] + mix([w[rows] for w in weights], late) * share_b[rows]
+        osend[first:last, :BLOCK] = mixed.reshape(last - first, BLOCK, HD)
+        for d in FAR_FIRST:
+            if first <= d < last:
+                put(osend.at[d], orecv.at[Z - d], B_SEND, B_RECV, along(d))
+
+    hand_out(4, 12)
+    hand_out(12, 16)
+    hand_out(0, 4)
 
     psend[...] = jnp.zeros_like(psend)
     loaded(suf, IN_SUF)

time: 47.8 us -> 47.7 us (level)
  no operation moved by 1% of the time
where the time goes in v7:
time: 47.7 us; the launch traced here: 47.6 us
  Pallas kernels  46.3 us (97%)
  between operations  0.66 us (1%)
  local copies, waits for them, and re-layouts  0.6 us (1%)
    pallas_call x1, Pallas kernels, local(): pl.pallas_call(kernel, out_shape=pltpu.VMEM((2, 8, 80), F32), in_specs=[p...  46.3 us

profile of v7, /device:TPU:1, one launch (start us, length us, event | category | flops | bytes accessed | tf_op | source)
XLA Modules:
  0.0 47.6 jit_solution(8947313314944649177)
XLA Ops:
  0.7 46.3 %shard_map.91 = f32[2,8,80]{2,1,0:T(8,128)S(1)} custom-call(f32[16,128]{1,0:T(8,128)} %bitcast.13, f32[256,128]{1,0:T(8,128)} %bitcast.9, f32[256,128]{1,0:T(8,128)} %bitcast.10, f32[128,128]{1,0:T(8,128)} %bitcast.11, f32[128,128]{1,0:T(8,128)} %bitcast.12, f32[2,128]{1,0:T(2,128)} %bitcast.14, f32[2,128]{1,0:T(2,128)} %bitcast.15, s32[1]{0:T(128)S(6)} %copy.12.len_in, ...), custom_call_target="tpu_custom_call" | custom-call | tf_op jit(solution)/shard_map/pallas_call | solution.py:281
  47.0 0.6 %copy.11 = f32[2,8,80]{2,1,0:T(8,128)} copy(f32[2,8,80]{2,1,0:T(8,128)S(1)} %shard_map.91) | data formatting | bytes 10240
